TPU v7x, 32 devices: a whole 2x2x4 slice. The times are simulated.
32 devices in a mesh: dom: 2 (over y), blk: 8 (over z, core), field: 2 (over x).
Axes of the slice: x: 2, y: 2, z: 4, core: 2. Of those that a mesh axis runs over, the one named last changes fastest.
Arguments:
- stiffness: bfloat16 [256, 27, 128, 128], P(('dom', 'blk'), None, 'field'), may hold values from -3 to 3
- prolong: bfloat16 [256, 2, 4096], P(('dom', 'blk'), 'field'), may hold values from -0.75 to 0.75
- columns: int32 [256, 27], P(('dom', 'blk')), may hold values from 0 to 19
- counts: int32 [16, 16], P(('dom', 'blk')), may hold values from 1 to 27, 256 in all within a row
- aggregate: int32 [256], P(('dom', 'blk')), may hold values from 0 to 4, as said below
- coarse_slots: int32 [256, 27], P(('dom', 'blk')), may hold values from 0 to 26
- requests: int32 [16, 2, 2], P(('dom', 'blk')), may hold values from 0 to 15
Outputs:
- coarse_matrix: bfloat16 [64, 27, 128, 128], P(('dom', 'blk'), None, 'field')
Inputs may be any that keep to these rules, and one draw needn't show every extreme that they name: `columns`: below 16 an entry names a row of the device itself; 16 + p * 2 + q names row q received from the device with dom index p. Each device's 16 counts sum to 256. The last fine row of every device has aggregate 4; all others lie below 4. `requests`: entry [g, p, q] is the row of device g that the device with dom index p receives in its place q.
All inputs are finite; a program needn't handle non-finite values.
Results may differ from a plain program's by a relative error of at most 0.0049.
Values may be sent and summed in bfloat16 or wider, within the bound.
No kernel may reach another device: no remote copies, remote signals or barrier semaphores. Data moves between devices by JAX's collectives and lax.ppermute only.
A program may use at most 128 MiB of HBM per device.

v0:
```python
import jax
import jax.numpy as jnp
from jax import lax
from jax.sharding import PartitionSpec as P

CSLOT = 27
NC_DEV = 4


def partner(value, axis, bit):
    mask = 2**bit
    pairs = [(source, source ^ mask) for source in range(lax.axis_size(axis))]
    return lax.ppermute(value, axis, pairs)


def shifted(x, axis, by):
    peers = lax.axis_size(axis)
    return lax.ppermute(x, axis, [(i, (i + by) % peers) for i in range(peers)])


def multiply(blocks, neighbour, fine_dofs, coarse):
    entries = blocks.shape[0]
    applied = jnp.einsum(
        "nagc,ngcb->nagb",
        blocks.reshape(entries, fine_dofs, 2, fine_dofs),
        neighbour,
        preferred_element_type=jnp.float32,
    )
    return applied.astype(jnp.bfloat16).reshape(entries, fine_dofs, 2 * coarse)


def shards(stiffness, prolong, columns, counts, aggregate, coarse_slots, requests):
    row_count = stiffness.shape[0]
    slot_count = stiffness.shape[1]
    fine_dofs = stiffness.shape[2]
    coarse = prolong.shape[2] // fine_dofs
    flat_size = fine_dofs * coarse
    own_flat = prolong[:, 0, :]
    outgoing = own_flat[requests[0]]
    ghosts = lax.all_to_all(outgoing, "dom", split_axis=0, concat_axis=0, tiled=True)
    own_field = jnp.concatenate([own_flat, ghosts.reshape(-1, flat_size)], axis=0)
    other_field = partner(own_field, "field", 0)
    is_first = lax.axis_index("field") == 0
    field_zero = jnp.where(is_first, own_field, other_field)
    field_one = jnp.where(is_first, other_field, own_field)
    extended = jnp.stack([field_zero, field_one], axis=1).reshape(-1, 2, fine_dofs, coarse)
    restrict = own_flat.reshape(row_count, fine_dofs, coarse)
    live_slot = jnp.arange(slot_count)[None, :] < counts[0][:, None]
    discard = (NC_DEV + 1) * CSLOT
    target = jnp.where(live_slot, aggregate[:, None] * CSLOT + coarse_slots, discard)
    entries = row_count * slot_count
    blocks = stiffness.reshape(entries, fine_dofs, 2 * fine_dofs)
    col_index = columns.reshape(-1)
    seg_index = target.reshape(-1)
    owner_row = jnp.arange(entries) // slot_count
    applied = multiply(blocks, extended[col_index], fine_dofs, coarse)
    contrib = jnp.einsum(
        "nca,ncb->nab", restrict[owner_row], applied, preferred_element_type=jnp.float32
    )
    contrib, seg_index = (contrib, seg_index)
    summed = jax.ops.segment_sum(contrib, seg_index, num_segments=discard)
    summed = summed.reshape(NC_DEV + 1, CSLOT, coarse, 2 * coarse)
    incoming = shifted(summed[NC_DEV].astype(jnp.bfloat16), "blk", 1).astype(jnp.float32)
    result = summed[:NC_DEV].at[0].add(incoming)
    return result.astype(jnp.bfloat16)


def solution(mesh):
    in_specs = (
        P(("dom", "blk"), None, "field", None),
        P(("dom", "blk"), "field", None),
        P(("dom", "blk"), None),
        P(("dom", "blk"), None),
        P(("dom", "blk")),
        P(("dom", "blk"), None),
        P(("dom", "blk"), None, None),
    )
    out_specs = P(("dom", "blk"), None, "field", None)
    return jax.shard_map(shards, mesh=mesh, in_specs=in_specs, out_specs=out_specs, check_vma=False)
```

profile of v0, /device:TPU:0, one launch (start us, length us, event | category | flops | bytes accessed | tf_op | source)
XLA Modules:
  0.0 182.3 jit_solution(12797593277903292621)
XLA Ops:
  0.0 0.7 compare_select_fusion.2
  0.8 1.5 gather_fusion.1
  2.3 0.6 reshape.170
  3.0 4.2 %all-to-all-start = ((bf16[2,2,4096]{2,1,0:T(2,128)(2,1)}), bf16[2,2,4096]{2,1,0:T(2,128)(2,1)S(1)}, u32[]{:S(2)}, u32[]{:S(2)}) async-start(bf16[2,2,4096]{2,1,0:T(2,128)(2,1)} %reshape.170), calls=%async_computation | async-start | bytes 65536 | tf_op jit(solution)/shard_map/all_to_all | solution.py:40
  7.2 0.8 reshape.159
  8.0 0.7 broadcast_multiply_fusion
  8.6 0.8 add_select_fusion
  9.4 1.7 all-to-all-done
  11.2 0.9 pad_maximum_fusion.1
  12.1 2.0 %collective-permute-start = (bf16[20,4096]{1,0:T(8,128)(2,1)S(1)}, bf16[20,4096]{1,0:T(8,128)(2,1)S(1)}, u32[]{:S(2)}, u32[]{:S(2)}) collective-permute-start(bf16[20,4096]{1,0:T(8,128)(2,1)S(1)} %pad_maximum_fusion.1), channel_id=1, source_target_pairs={{0,1},{1,0},{2,3},{3,2},{4,5},{5,4},{6,7},{7,6},{8,9},{9,8},{10,11... | collective-permute-start | bytes 491528 | tf_op jit(solution)/shard_map/ppermute | solution.py:13
  14.1 1.2 reshape_squeeze.3
  15.3 23.9 %reshape_reshape.3 = bf16[432,64,2,64]{3,2,1,0:T(2,128)(2,1)} reshape(bf16[16,27,64,128]{3,2,1,0:T(8,128)(2,1)} %param.9) | data formatting | bytes 14155776 | tf_op jit(solution)/shard_map/reshape;reshape | solution.py:25
  39.3 13.3 %gather_fusion = bf16[432,64,64]{2,1,0:T(8,128)(2,1)} fusion(bf16[16,64,64]{2,1,0:T(8,128)(2,1)S(1)} %reshape_squeeze.3, s32[1024]{0:T(1024)S(1)} %pad_clamp_fusion.2), kind=kCustom, calls=%fused_computation | custom fusion | bytes 7079616 | tf_op jit(solution)/shard_map/gather | solution.py:58
  52.8 0.3 stack.9
  53.1 0.3 stack.10
  53.6 13.1 %gather_fusion.2 = bf16[432,2,64,64]{3,2,1,0:T(8,128)(2,1)} fusion(bf16[20,2,64,64]{3,2,1,0:T(8,128)(2,1)S(1)} %pad_maximum_fusion, s32[1024]{0:T(1024)S(1)} %pad_clamp_fusion), kind=kCustom, calls=%fused_computation.2 | custom fusion | bytes 14157504 | tf_op jit(solution)/shard_map/gather | solution.py:56
  66.7 18.4 %fusion.2 = bf16[432,2,64,64]{3,2,1,0:T(8,128)(2,1)} fusion(bf16[432,2,64,64]{3,2,1,0:T(8,128)(2,1)} %gather_fusion.2, bf16[432,64,2,64]{3,2,1,0:T(2,128)(2,1)} %reshape_reshape.3), kind=kOutput, calls=%fused_computation.6 | convolution fusion | flops 456523776 | bytes 21233664 | tf_op jit(solution)/shard_map/nagc,ngcb->nagb/dot_general | solution.py:23
  85.1 16.6 %fusion.7 = f32[432,64,128]{2,1,0:T(8,128)} fusion(bf16[432,64,64]{2,1,0:T(8,128)(2,1)} %gather_fusion, bf16[432,64,128]{1,2,0:T(8,128)(2,1)} %bitcast.25), kind=kOutput, calls=%fused_computation.28 | convolution fusion | flops 452984832 | bytes 24772608 | tf_op jit(solution)/shard_map/nca,ncb->nab/dot_general | solution.py:57
  101.7 2.6 %broadcast_in_dim.6 = f32[135,64,128]{2,1,0:T(8,128)} broadcast(f32[]{:T(128)} %constant.45.clone.1), dimensions={} | broadcast | bytes 4423684 | tf_op jit(solution)/shard_map/broadcast_in_dim | solution.py:61
  104.3 65.1 %scatter_fusion = f32[135,64,128]{2,1,0:T(8,128)} fusion(f32[135,64,128]{2,1,0:T(8,128)} %broadcast_in_dim.6, s32[432]{0:T(512)S(1)} %reshape.187, f32[432,64,128]{2,1,0:T(8,128)} %fusion.7), kind=kCustom, calls=%fused_computation.3 | custom fusion | flops 3538944 | bytes 42469056 | tf_op jit(solution)/shard_map/scatter-add | solution.py:61
  169.4 1.2 slice.59
  170.7 3.6 %slice.50 = bf16[108,64,128]{2,1,0:T(8,128)(2,1)} slice(f32[135,64,128]{2,1,0:T(8,128)} %scatter_fusion), slice={[0:108], [0:64], [0:128]} | slice | bytes 3538944 | tf_op jit(solution)/shard_map/slice | solution.py:64
  174.3 5.9 %collective-permute-done.1 = bf16[27,64,128]{2,1,0:T(8,128)(2,1)S(1)} collective-permute-done((bf16[27,64,128]{2,1,0:T(8,128)(2,1)S(1)}, bf16[27,64,128]{2,1,0:T(8,128)(2,1)S(1)}, u32[]{:S(2)}, u32[]{:S(2)}) %collective-permute-start.1) | collective-permute-done | bytes 442400 | tf_op jit(solution)/shard_map/ppermute | solution.py:18
  180.2 2.1 %fusion.6 = bf16[4,27,64,128]{3,2,1,0:T(8,128)(2,1)} fusion(bf16[4,27,64,128]{3,2,1,0:T(8,128)(2,1)} %bitcast.29, f32[135,64,128]{2,1,0:T(8,128)} %scatter_fusion, bf16[27,64,128]{2,1,0:T(8,128)(2,1)S(1)} %collective-permute-done.1), kind=kLoop, calls=%fused_computation.10 | loop fusion | flops 442368 | bytes 2211840 | tf_op jit(solution)/shard_map/scatter-add | solution.py:64
  (14 shorter events, 0.5 us)
Async XLA Ops:
  3.0 8.2 %all-to-all-start = ((bf16[2,2,4096]{2,1,0:T(2,128)(2,1)}), bf16[2,2,4096]{2,1,0:T(2,128)(2,1)S(1)}, u32[]{:S(2)}, u32[]{:S(2)}) async-start(bf16[2,2,4096]{2,1,0:T(2,128)(2,1)} %reshape.170), calls=%async_computation | async-start | bytes 65536 | tf_op jit(solution)/shard_map/all_to_all | solution.py:40
  12.1 40.6 %collective-permute-start = (bf16[20,4096]{1,0:T(8,128)(2,1)S(1)}, bf16[20,4096]{1,0:T(8,128)(2,1)S(1)}, u32[]{:S(2)}, u32[]{:S(2)}) collective-permute-start(bf16[20,4096]{1,0:T(8,128)(2,1)S(1)} %pad_maximum_fusion.1), channel_id=1, source_target_pairs={{0,1},{1,0},{2,3},{3,2},{4,5},{5,4},{6,7},{7,6},{8,9},{9,8},{10,11... | collective-permute-start | bytes 491528 | tf_op jit(solution)/shard_map/ppermute | solution.py:13
  15.3 37.4 %copy-start = (bf16[16,1,4096]{2,0,1:T(8,128)(2,1)S(1)}, bf16[16,1,4096]{2,0,1:T(8,128)(2,1)}, u32[]{:S(2)}) copy-start(bf16[16,1,4096]{2,0,1:T(8,128)(2,1)} %param.10) | copy-start | bytes 393220
  170.7 9.6 %collective-permute-start.1 = (bf16[27,64,128]{2,1,0:T(8,128)(2,1)S(1)}, bf16[27,64,128]{2,1,0:T(8,128)(2,1)S(1)}, u32[]{:S(2)}, u32[]{:S(2)}) collective-permute-start(bf16[27,64,128]{2,1,0:T(8,128)(2,1)S(1)} %slice.59), channel_id=1, source_target_pairs={{0,2},{2,4},{4,6},{6,8},{8,10},{10,12},{12,14},{14,0},{1,3},{3,5},... | collective-permute-start | bytes 1327112 | tf_op jit(solution)/shard_map/ppermute | solution.py:18
where the time goes:
time: 184 us; the launch traced here: 182 us
  other arithmetic  70.5 us (38%)
  local copies, waits for them, and re-layouts  62.8 us (34%)
  matrix products  35 us (19%)
  waiting for transfers between devices  7.6 us (4%)
  starting transfers between devices  6.31 us (3%)
    scatter-add x1, other arithmetic, shards(): summed = jax.ops.segment_sum(contrib, seg_index, num_segments=discard)  65.1 us
    another operation x1, local copies, waits for them, and re-layouts, multiply(): blocks.reshape(entries, fine_dofs, 2, fine_dofs)  23.9 us
    dot_general x1, matrix products, multiply(): jnp.einsum('nagc,ngcb->nagb', blocks.reshape(entries, fine_dofs, 2, fine_...  18.4 us
    dot_general x1, matrix products, shards(): jnp.einsum('nca,ncb->nab', restrict[owner_row], applied, preferred_elemen...  16.6 us
    gather x1, local copies, waits for them, and re-layouts, shards(): restrict[owner_row]  13.3 us
    gather x1, local copies, waits for them, and re-layouts, shards(): applied = multiply(blocks, extended[col_index], fine_dofs, coarse)  13.1 us
    ppermute x1, waiting for transfers between devices, shifted(): return lax.ppermute(x, axis, [(i, (i + by) % peers) for i in range(peers)])  5.89 us
    all_to_all x1, starting transfers between devices, shards(): lax.all_to_all(outgoing, 'dom', split_axis=0, concat_axis=0, tiled=True)  4.23 us
  transfers between devices with their start and end apart: 3, of which 2 were waited for; matrix products, arithmetic and copies ran while one was open for 24% of the time, Pallas kernels for 0%

commit v1 on v0

v1 whole, which is shorter than its diff:
```python
import functools

import jax
import jax.numpy as jnp
from jax import lax
from jax.experimental import pallas as pl
from jax.experimental.pallas import tpu as pltpu
from jax.sharding import PartitionSpec as P

CSLOT = 27
NC_DEV = 4
UNROLL = 9

VMEM = pltpu.VMEM
SMEM = pltpu.SMEM
f32 = jnp.float32
bf16 = jnp.bfloat16


def in_vmem(x):
    return pltpu.with_memory_space_constraint(x, VMEM)


def spec(space):
    return pl.BlockSpec(memory_space=space)


def shift_pairs(n, by):
    return [(i, (i + by) % n) for i in range(n)]


def pick_kernel(n_dom, q, requests, flat, out):
    me = lax.axis_index("dom")
    rows = flat.shape[0]
    lane = lax.broadcasted_iota(jnp.int32, (1, rows), 1)
    hot = []
    for s in range(1, n_dom):
        to = lax.rem(me + s, n_dom)
        for r in range(q):
            hot.append((lane == requests[0, to, r]).astype(f32))
    hot = jnp.concatenate(hot, axis=0).astype(bf16)
    out[...] = jnp.dot(hot, flat[...], preferred_element_type=f32).astype(bf16)


def pick(requests, flat, n_dom, q):
    return pl.pallas_call(
        functools.partial(pick_kernel, n_dom, q),
        out_shape=VMEM(((n_dom - 1) * q, flat.shape[1]), bf16),
        in_specs=[spec(SMEM), spec(VMEM)],
        out_specs=spec(VMEM),
    )(requests, flat)


def entries(base, count, live, columns, slots, row, stiff, restrict, table, acc, offset, trash):
    applied = []
    for u in range(count):
        k = base + u
        j = columns[row, k]
        x = jnp.dot(stiff[k], table[j], preferred_element_type=f32)
        applied.append(x.astype(bf16))
    for u in range(0, count, 2):
        pair = applied[u : u + 2]
        x = jnp.concatenate(pair, axis=1) if len(pair) == 2 else pair[0]
        z = jnp.dot(restrict, x, preferred_element_type=f32)
        for h in range(len(pair)):
            k = base + u + h
            seg = jnp.where(k < live, offset + slots[row, k], trash)
            acc[seg] += z[:, h * 128 : h * 128 + 128]


def spill_kernel(n_dom, q, columns, counts, slots, requests, stiffness, own, other, g_own, g_other,
                 table, out, row_buf, acc, sem):
    rows, slot_count = stiffness.shape[:2]
    last = rows - 1
    copy = pltpu.make_async_copy(stiffness.at[last], row_buf, sem)
    copy.start()
    first = lax.axis_index("field") == 0
    me = lax.axis_index("dom")
    dofs = own.shape[1]

    def put(j, mine, theirs):
        zero = jnp.zeros((dofs, dofs), bf16)
        top = jnp.where(first, mine, theirs)
        bottom = jnp.where(first, theirs, mine)
        table[j] = jnp.concatenate(
            [jnp.concatenate([top, zero], axis=1), jnp.concatenate([zero, bottom], axis=1)], axis=0)

    for j in range(rows):
        put(j, own[j], other[j])
    for s in range(1, n_dom):
        source = lax.rem(me + n_dom - s, n_dom)
        for r in range(q):
            put(rows + source * q + r, g_own[(s - 1) * q + r], g_other[(s - 1) * q + r])
    for r in range(q):
        table[rows + me * q + r] = table[requests[0, me, r]]
    acc[...] = jnp.zeros_like(acc)
    copy.wait()
    live = counts[0, last]
    restrict = own[last].T
    for c in range(slot_count // UNROLL):
        @pl.when(c * UNROLL < live)
        def _():
            entries(c * UNROLL, UNROLL, live, columns, slots, last, row_buf, restrict, table, acc, 0, CSLOT)
    out[...] = acc[0:CSLOT].astype(bf16)


def main_kernel(columns, counts, aggregate, slots, stiffness, own, table, out, first_row, stiff, acc, stage, sems, out_sem):
    rows, slot_count = stiffness.shape[:2]
    last = rows - 1
    for i in range(last):
        pltpu.make_async_copy(stiffness.at[i], stiff.at[i], sems.at[i]).start()
    acc[...] = jnp.zeros_like(acc)

    @pl.loop(0, last)
    def _(i):
        pltpu.make_async_copy(stiffness.at[i], stiff.at[i], sems.at[i]).wait()
        live = counts[0, i]
        restrict = own[i].T
        offset = aggregate[i] * CSLOT

        @pl.loop(0, (live + (UNROLL - 1)) // UNROLL)
        def _(c):
            entries(c * UNROLL, UNROLL, live, columns, slots, i, stiff.at[i], restrict, table, acc,
                    offset, NC_DEV * CSLOT)

    first_row[...] = acc[0:CSLOT]
    for c in range(1, NC_DEV):
        stage[c - 1] = acc[c * CSLOT : (c + 1) * CSLOT].astype(bf16)
    copy = pltpu.make_async_copy(stage, out.at[1:NC_DEV], out_sem)
    copy.start()
    copy.wait()


def final_kernel(partial, incoming, _, out, stage, sem):
    stage[...] = (partial[...] + incoming[...].astype(f32)).astype(bf16)
    copy = pltpu.make_async_copy(stage, out.at[0], sem)
    copy.start()
    copy.wait()


def shards(stiffness, prolong, columns, counts, aggregate, coarse_slots, requests):
    rows, slot_count, dofs, width = stiffness.shape
    coarse = prolong.shape[2] // dofs
    n_dom = lax.axis_size("dom")
    n_field = lax.axis_size("field")
    q = requests.shape[2]
    own_flat = prolong[:, 0, :]
    other_flat = lax.ppermute(own_flat, "field", [(0, 1), (1, 0)])
    picked = pick(requests, own_flat, n_dom, q)
    g_own, g_other = [], []
    for s in range(1, n_dom):
        part = picked[(s - 1) * q : s * q]
        g_own.append(lax.ppermute(part, "dom", shift_pairs(n_dom, s)))
        pairs = [(d * n_field + f, ((d + s) % n_dom) * n_field + 1 - f) for d in range(n_dom) for f in range(n_field)]
        g_other.append(lax.ppermute(part, ("dom", "field"), pairs))
    g_own = jnp.concatenate(g_own, axis=0)
    g_other = jnp.concatenate(g_other, axis=0)
    as_blocks = lambda x: x.reshape(x.shape[0], dofs, coarse)
    own, other = as_blocks(own_flat), as_blocks(other_flat)
    g_own, g_other = as_blocks(g_own), as_blocks(g_other)
    n_ext = rows + n_dom * q
    limit = pltpu.CompilerParams(vmem_limit_bytes=40 * 2**20)
    table, spill = pl.pallas_call(
        functools.partial(spill_kernel, n_dom, q),
        out_shape=(VMEM((n_ext, width, 2 * coarse), bf16), VMEM((CSLOT, dofs, 2 * coarse), bf16)),
        in_specs=[spec(SMEM)] * 4 + [spec(pl.ANY)] + [spec(VMEM)] * 4,
        out_specs=(spec(VMEM), spec(VMEM)),
        scratch_shapes=[VMEM((slot_count, dofs, width), bf16), VMEM((CSLOT + 1, coarse, 2 * coarse), f32),
                        pltpu.SemaphoreType.DMA(())],
        compiler_params=limit,
        cost_estimate=pl.CostEstimate(flops=10**7, bytes_accessed=10**6, transcendentals=0),
    )(columns, counts, coarse_slots, requests, stiffness, in_vmem(own), in_vmem(other), in_vmem(g_own), in_vmem(g_other))
    incoming = lax.ppermute(spill, "blk", shift_pairs(lax.axis_size("blk"), 1))
    out_shape = jax.ShapeDtypeStruct((NC_DEV, CSLOT, coarse, 2 * coarse), bf16)
    out, partial = pl.pallas_call(
        main_kernel,
        out_shape=(out_shape, VMEM((CSLOT, coarse, 2 * coarse), f32)),
        in_specs=[spec(SMEM)] * 4 + [spec(pl.ANY)] + [spec(VMEM)] * 2,
        out_specs=(spec(pl.ANY), spec(VMEM)),
        scratch_shapes=[VMEM((rows, slot_count, dofs, width), bf16),
                        VMEM((NC_DEV * CSLOT + 1, coarse, 2 * coarse), f32),
                        VMEM((NC_DEV - 1, CSLOT, coarse, 2 * coarse), bf16),
                        pltpu.SemaphoreType.DMA((rows,)), pltpu.SemaphoreType.DMA(())],
        compiler_params=limit,
        cost_estimate=pl.CostEstimate(flops=10**9, bytes_accessed=10**7, transcendentals=0),
    )(columns, counts, aggregate, coarse_slots, stiffness, in_vmem(own), in_vmem(table))
    return pl.pallas_call(
        final_kernel,
        out_shape=out_shape,
        in_specs=[spec(VMEM), spec(VMEM), spec(pl.ANY)],
        out_specs=spec(pl.ANY),
        scratch_shapes=[VMEM((CSLOT, coarse, 2 * coarse), bf16), pltpu.SemaphoreType.DMA(())],
        input_output_aliases={2: 0},
        compiler_params=limit,
    )(in_vmem(partial), in_vmem(incoming), out)


def solution(mesh):
    in_specs = (
        P(("dom", "blk"), None, "field", None),
        P(("dom", "blk"), "field", None),
        P(("dom", "blk"), None),
        P(("dom", "blk"), None),
        P(("dom", "blk")),
        P(("dom", "blk"), None),
        P(("dom", "blk"), None, None),
    )
    out_specs = P(("dom", "blk"), None, "field", None)
    return jax.shard_map(shards, mesh=mesh, in_specs=in_specs, out_specs=out_specs, check_vma=False)
```

time: 184 us -> 38.4 us (0.21)
  the two profiles are of different devices: /device:TPU:0 before, /device:TPU:1 now
where the time goes in v1:
time: 38.4 us; the launch traced here: 37.8 us
  Pallas kernels  22.1 us (58%)
  local copies, waits for them, and re-layouts  7.36 us (19%)
  starting transfers between devices  7.02 us (18%)
  waiting for transfers between devices  1.23 us (3%)
    pallas_call x1, Pallas kernels, shards(): pl.pallas_call(main_kernel, out_shape=(out_shape, VMEM((CSLOT, coarse, 2...  17.7 us
    unnamed x18, local copies, waits for them, and re-layouts  5.75 us
    ppermute x1, starting transfers between devices, shards(): incoming = lax.ppermute(spill, 'blk', shift_pairs(lax.axis_size('blk'), 1))  3.6 us
    pallas_call x1, Pallas kernels, shards(): pl.pallas_call(functools.partial(spill_kernel, n_dom, q), out_shape=(VMEM...  2.43 us
    ppermute x1, starting transfers between devices, shards(): other_flat = lax.ppermute(own_flat, 'field', [(0, 1), (1, 0)])  2.04 us
    ppermute x1, starting transfers between devices, shards(): g_other.append(lax.ppermute(part, ('dom', 'field'), pairs))  1.28 us
    another operation x1, local copies, waits for them, and re-layouts, shards(): as_blocks = lambda x: x.reshape(x.shape[0], dofs, coarse)  1.18 us
    ppermute x1, waiting for transfers between devices, shards(): g_other.append(lax.ppermute(part, ('dom', 'field'), pairs))  1.16 us
  transfers between devices with their start and end apart: 4, of which 2 were waited for; matrix products, arithmetic and copies ran while one was open for 4% of the time, Pallas kernels for 50%

profile of v1, /device:TPU:1, one launch (start us, length us, event | category | flops | bytes accessed | tf_op | source)
XLA Modules:
  0.0 37.8 jit_solution(13317895292760794610)
XLA Ops:
  0.0 2.0 %collective-permute-start = (bf16[16,4096]{1,0:T(8,128)(2,1)}, bf16[16,4096]{1,0:T(8,128)(2,1)S(1)}, u32[]{:S(2)}, u32[]{:S(2)}) collective-permute-start(bf16[16,4096]{1,0:T(8,128)(2,1)} %bitcast.3), channel_id=1, source_target_pairs={{0,1},{1,0},{2,3},{3,2},{4,5},{5,4},{6,7},{7,6},{8,9},{9,8},{10,11... | collective-permute-start | bytes 393224 | tf_op jit(solution)/shard_map/ppermute | solution.py:148
  2.0 1.1 %shard_map.73 = bf16[2,4096]{1,0:T(2,128)(2,1)S(1)} custom-call(s32[1,2,2]{2,1,0:T(2,128)} %requests.3, bf16[16,4096]{1,0:T(8,128)(2,1)} %bitcast.4), custom_call_target="tpu_custom_call" | custom-call | tf_op jit(solution)/shard_map/pallas_call | solution.py:46
  3.2 1.3 %collective-permute-start.2 = (bf16[2,4096]{1,0:T(2,128)(2,1)S(1)}, bf16[2,4096]{1,0:T(2,128)(2,1)S(1)}, u32[]{:S(2)}, u32[]{:S(2)}) collective-permute-start(bf16[2,4096]{1,0:T(2,128)(2,1)S(1)} %shard_map.73), channel_id=1, source_target_pairs={{0,17},{1,16},{16,1},{17,0},{2,19},{3,18},{18,3},{19,2},{4,21},{5,... | collective-permute-start | bytes 49160 | tf_op jit(solution)/shard_map/ppermute | solution.py:155
  4.4 0.1 collective-permute-start.1
  4.5 1.2 %reshape_squeeze.3.own = bf16[16,64,64]{2,1,0:T(8,128)(2,1)S(1)} reshape(bf16[16,1,4096]{2,0,1:T(8,128)(2,1)} %param.8) | data formatting | bytes 262144 | tf_op jit(solution)/shard_map/reshape;squeeze | solution.py:158
  5.7 1.2 %collective-permute-done.2 = bf16[2,4096]{1,0:T(2,128)(2,1)S(1)} collective-permute-done((bf16[2,4096]{1,0:T(2,128)(2,1)S(1)}, bf16[2,4096]{1,0:T(2,128)(2,1)S(1)}, u32[]{:S(2)}, u32[]{:S(2)}) %collective-permute-start.2) | collective-permute-done | bytes 16416 | tf_op jit(solution)/shard_map/ppermute | solution.py:155
  6.9 0.1 reshape.11.g_other
  7.0 0.1 collective-permute-done.1
  7.0 0.1 reshape.10.g_own
  7.1 0.0 collective-permute-done
  7.2 0.2 reshape.9.other
  7.4 0.0 copy-start
  7.4 3.0 %copy-done = bf16[16,27,64,128]{3,2,1,0:T(8,128)(2,1)S(1)} copy-done((bf16[16,27,64,128]{3,2,1,0:T(8,128)(2,1)S(1)}, bf16[16,27,64,128]{3,2,1,0:T(8,128)(2,1)}, u32[]{:S(2)}) %copy-start) | copy-done | bytes 7077912
  10.4 0.7 %copy-done.2 = s32[16,27]{1,0:T(8,128)S(1)} copy-done((s32[16,27]{1,0:T(8,128)S(1)}, s32[16,27]{1,0:T(8,128)}, u32[]{:S(2)}) %copy-start.2) | copy-done | bytes 1752
  11.1 0.7 %copy-done.4 = s32[16,27]{1,0:T(8,128)S(1)} copy-done((s32[16,27]{1,0:T(8,128)S(1)}, s32[16,27]{1,0:T(8,128)}, u32[]{:S(2)}) %copy-start.4) | copy-done | bytes 1752
  11.8 0.7 %copy-done.6 = s32[1,2,2]{2,1,0:T(2,128)S(1)} copy-done((s32[1,2,2]{2,1,0:T(2,128)S(1)}, s32[1,2,2]{2,1,0:T(2,128)}, u32[]{:S(2)}) %copy-start.6) | copy-done | bytes 40
  12.5 0.7 %copy-done.7 = s32[1,16]{1,0:T(1,128)S(1)} copy-done((s32[1,16]{1,0:T(1,128)S(1)}, s32[1,16]{1,0:T(1,128)}, u32[]{:S(2)}) %copy-start.7) | copy-done | bytes 88
  13.2 2.4 %shard_map.74 = (bf16[20,128,128]{2,1,0:T(8,128)(2,1)S(1)}, bf16[27,64,128]{2,1,0:T(8,128)(2,1)S(1)}) custom-call(s32[16,27]{1,0:T(8,128)S(1)} %copy-done.2, s32[1,16]{1,0:T(1,128)S(1)} %copy-done.7, s32[16,27]{1,0:T(8,128)S(1)} %copy-done.4, s32[1,2,2]{2,1,0:T(2,128)S(1)} %copy-done.6, bf16[16,27,64,128]{3,2,1,0:T(8,128)(2,1)S(1)} %copy-done, ...), custom_call_target="tpu_custom_call" | custom-call | flops 10000000 | bytes 1000000 | tf_op jit(solution)/shard_map/pallas_call | solution.py:163
  15.6 3.6 %collective-permute-start.3 = (bf16[27,64,128]{2,1,0:T(8,128)(2,1)S(1)}, bf16[27,64,128]{2,1,0:T(8,128)(2,1)S(1)}, u32[]{:S(2)}, u32[]{:S(2)}) collective-permute-start(bf16[27,64,128]{2,1,0:T(8,128)(2,1)S(1)} %get-tuple-element.11), channel_id=1, source_target_pairs={{0,2},{2,4},{4,6},{6,8},{8,10},{10,12},{12,14},{14,0},{1,3},{3,5},... | collective-permute-start | bytes 1327112 | tf_op jit(solution)/shard_map/ppermute | solution.py:173
  19.2 0.0 copy-done.1
  19.2 0.0 copy-done.8
  19.2 17.7 %shard_map.75 = (bf16[4,27,64,128]{3,2,1,0:T(8,128)(2,1)}, f32[27,64,128]{2,1,0:T(8,128)S(1)}) custom-call(s32[16,27]{1,0:T(8,128)S(1)} %copy-done.3, s32[1,16]{1,0:T(1,128)S(1)} %copy-done.7, s32[16]{0:T(128)S(1)} %copy-done.8, s32[16,27]{1,0:T(8,128)S(1)} %copy-done.5, bf16[16,27,64,128]{3,2,1,0:T(8,128)(2,1)S(1)} %copy-done.1, ...), custom_call_target="tpu_custom_call" | custom-call | flops 1000000000 | bytes 10000000 | tf_op jit(solution)/shard_map/pallas_call | solution.py:175
  36.9 0.0 collective-permute-done.3.incoming
  36.9 0.9 %shard_map.76 = bf16[4,27,64,128]{3,2,1,0:T(8,128)(2,1)} custom-call(f32[27,64,128]{2,1,0:T(8,128)S(1)} %get-tuple-element.10.partial, bf16[27,64,128]{2,1,0:T(8,128)(2,1)S(1)} %collective-permute-done.3.incoming, bf16[4,27,64,128]{3,2,1,0:T(8,128)(2,1)} %get-tuple-element.12._), custom_call_target="tpu_custom_call", output_to_operand_aliasing={{}: (2, {})} | custom-call | tf_op jit(solution)/shard_map/pallas_call | solution.py:187
  (10 shorter events, 0.0 us)
Async XLA Ops:
  0.0 7.1 %collective-permute-start = (bf16[16,4096]{1,0:T(8,128)(2,1)}, bf16[16,4096]{1,0:T(8,128)(2,1)S(1)}, u32[]{:S(2)}, u32[]{:S(2)}) collective-permute-start(bf16[16,4096]{1,0:T(8,128)(2,1)} %bitcast.3), channel_id=1, source_target_pairs={{0,1},{1,0},{2,3},{3,2},{4,5},{5,4},{6,7},{7,6},{8,9},{9,8},{10,11... | collective-permute-start | bytes 393224 | tf_op jit(solution)/shard_map/ppermute | solution.py:148
  3.2 3.7 %collective-permute-start.2 = (bf16[2,4096]{1,0:T(2,128)(2,1)S(1)}, bf16[2,4096]{1,0:T(2,128)(2,1)S(1)}, u32[]{:S(2)}, u32[]{:S(2)}) collective-permute-start(bf16[2,4096]{1,0:T(2,128)(2,1)S(1)} %shard_map.73), channel_id=1, source_target_pairs={{0,17},{1,16},{16,1},{17,0},{2,19},{3,18},{18,3},{19,2},{4,21},{5,... | collective-permute-start | bytes 49160 | tf_op jit(solution)/shard_map/ppermute | solution.py:155
  4.4 2.6 %collective-permute-start.1 = (bf16[2,4096]{1,0:T(2,128)(2,1)S(1)}, bf16[2,4096]{1,0:T(2,128)(2,1)S(1)}, u32[]{:S(2)}, u32[]{:S(2)}) collective-permute-start(bf16[2,4096]{1,0:T(2,128)(2,1)S(1)} %shard_map.73), channel_id=1, source_target_pairs={{0,16},{16,0},{1,17},{17,1},{2,18},{18,2},{3,19},{19,3},{4,20},{20... | collective-permute-start | bytes 49160 | tf_op jit(solution)/shard_map/ppermute | solution.py:153
  7.4 3.0 %copy-start = (bf16[16,27,64,128]{3,2,1,0:T(8,128)(2,1)S(1)}, bf16[16,27,64,128]{3,2,1,0:T(8,128)(2,1)}, u32[]{:S(2)}) copy-start(bf16[16,27,64,128]{3,2,1,0:T(8,128)(2,1)} %stiffness.3) | copy-start | bytes 21233668
  10.4 0.7 %copy-start.2 = (s32[16,27]{1,0:T(8,128)S(1)}, s32[16,27]{1,0:T(8,128)}, u32[]{:S(2)}) copy-start(s32[16,27]{1,0:T(8,128)} %columns.3) | copy-start | bytes 5188
  11.1 0.7 %copy-start.4 = (s32[16,27]{1,0:T(8,128)S(1)}, s32[16,27]{1,0:T(8,128)}, u32[]{:S(2)}) copy-start(s32[16,27]{1,0:T(8,128)} %slots.3) | copy-start | bytes 5188
  11.8 0.7 %copy-start.6 = (s32[1,2,2]{2,1,0:T(2,128)S(1)}, s32[1,2,2]{2,1,0:T(2,128)}, u32[]{:S(2)}) copy-start(s32[1,2,2]{2,1,0:T(2,128)} %requests.3) | copy-start | bytes 52
  12.5 0.7 %copy-start.7 = (s32[1,16]{1,0:T(1,128)S(1)}, s32[1,16]{1,0:T(1,128)}, u32[]{:S(2)}) copy-start(s32[1,16]{1,0:T(1,128)} %counts.3) | copy-start | bytes 196
  13.1 6.1 %copy-start.1 = (bf16[16,27,64,128]{3,2,1,0:T(8,128)(2,1)S(1)}, bf16[16,27,64,128]{3,2,1,0:T(8,128)(2,1)}, u32[]{:S(2)}) copy-start(bf16[16,27,64,128]{3,2,1,0:T(8,128)(2,1)} %stiffness.3) | copy-start | bytes 21233668
  13.1 6.1 %copy-start.3 = (s32[16,27]{1,0:T(8,128)S(1)}, s32[16,27]{1,0:T(8,128)}, u32[]{:S(2)}) copy-start(s32[16,27]{1,0:T(8,128)} %columns.3) | copy-start | bytes 5188
  13.2 6.1 %copy-start.5 = (s32[16,27]{1,0:T(8,128)S(1)}, s32[16,27]{1,0:T(8,128)}, u32[]{:S(2)}) copy-start(s32[16,27]{1,0:T(8,128)} %slots.3) | copy-start | bytes 5188
  13.2 6.1 %copy-start.8 = (s32[16]{0:T(128)S(1)}, s32[16]{0:T(128)}, u32[]{:S(2)}) copy-start(s32[16]{0:T(128)} %aggregate.1) | copy-start | bytes 196
  15.6 21.3 %collective-permute-start.3 = (bf16[27,64,128]{2,1,0:T(8,128)(2,1)S(1)}, bf16[27,64,128]{2,1,0:T(8,128)(2,1)S(1)}, u32[]{:S(2)}, u32[]{:S(2)}) collective-permute-start(bf16[27,64,128]{2,1,0:T(8,128)(2,1)S(1)} %get-tuple-element.11), channel_id=1, source_target_pairs={{0,2},{2,4},{4,6},{6,8},{8,10},{10,12},{12,14},{14,0},{1,3},{3,5},... | collective-permute-start | bytes 1327112 | tf_op jit(solution)/shard_map/ppermute | solution.py:173

commit v2 on v1

--- a/solution.py
+++ b/solution.py
@@ -9,7 +9,10 @@
 
 CSLOT = 27
 NC_DEV = 4
-UNROLL = 9
+AVGNZ = 16
+UNROLL = 32
+COLUMN_BIT = 10
+SEG_BIT = 16
 
 VMEM = pltpu.VMEM
 SMEM = pltpu.SMEM
@@ -19,6 +22,10 @@
 
 def in_vmem(x):
     return pltpu.with_memory_space_constraint(x, VMEM)
+
+
+def in_hbm(x):
+    return pltpu.with_memory_space_constraint(x, pltpu.HBM)
 
 
 def spec(space):
@@ -51,32 +58,28 @@
     )(requests, flat)
 
 
-def entries(base, count, live, columns, slots, row, stiff, restrict, table, acc, offset, trash):
-    applied = []
-    for u in range(count):
-        k = base + u
-        j = columns[row, k]
-        x = jnp.dot(stiff[k], table[j], preferred_element_type=f32)
-        applied.append(x.astype(bf16))
-    for u in range(0, count, 2):
-        pair = applied[u : u + 2]
-        x = jnp.concatenate(pair, axis=1) if len(pair) == 2 else pair[0]
-        z = jnp.dot(restrict, x, preferred_element_type=f32)
-        for h in range(len(pair)):
-            k = base + u + h
-            seg = jnp.where(k < live, offset + slots[row, k], trash)
-            acc[seg] += z[:, h * 128 : h * 128 + 128]
-
-
-def spill_kernel(n_dom, q, columns, counts, slots, requests, stiffness, own, other, g_own, g_other,
-                 table, out, row_buf, acc, sem):
-    rows, slot_count = stiffness.shape[:2]
-    last = rows - 1
-    copy = pltpu.make_async_copy(stiffness.at[last], row_buf, sem)
-    copy.start()
+def list_kernel(columns, counts, aggregate, slots, out, packed_v, packed, sem):
+    rows, slot_count = columns.shape
+    block = lax.broadcasted_iota(jnp.int32, (rows, slot_count), 0) * slot_count
+    block = block + lax.broadcasted_iota(jnp.int32, (rows, slot_count), 1)
+    packed_v[0:rows, 0:slot_count] = block + (columns[...] << COLUMN_BIT) + (slots[...] << SEG_BIT)
+    copy = pltpu.make_async_copy(packed_v, packed, sem)
+    copy.start()
+    copy.wait()
+    base = 0
+    for i in range(rows - 1):
+        offset = (aggregate[i] * CSLOT) << SEG_BIT
+        for k in range(slot_count):
+            out[base + k] = packed[i, k] + offset
+        base = base + counts[0, i]
+    for k in range(slot_count):
+        out[base + k] = (NC_DEV * CSLOT) << SEG_BIT
+
+
+def table_of(n_dom, q, requests, own, other, g_own, g_other, table):
+    rows, dofs = own.shape[:2]
     first = lax.axis_index("field") == 0
     me = lax.axis_index("dom")
-    dofs = own.shape[1]
 
     def put(j, mine, theirs):
         zero = jnp.zeros((dofs, dofs), bf16)
@@ -93,36 +96,57 @@
             put(rows + source * q + r, g_own[(s - 1) * q + r], g_other[(s - 1) * q + r])
     for r in range(q):
         table[rows + me * q + r] = table[requests[0, me, r]]
+
+
+def spill_kernel(n_dom, q, columns, counts, slots, requests, stiffness, own, other, g_own, g_other,
+                 table, out, row_buf, acc, sem):
+    rows, slot_count = stiffness.shape[:2]
+    last = rows - 1
+    copy = pltpu.make_async_copy(stiffness.at[last], row_buf, sem)
+    copy.start()
+    table_of(n_dom, q, requests, own, other, g_own, g_other, table)
     acc[...] = jnp.zeros_like(acc)
-    copy.wait()
     live = counts[0, last]
     restrict = own[last].T
-    for c in range(slot_count // UNROLL):
-        @pl.when(c * UNROLL < live)
-        def _():
-            entries(c * UNROLL, UNROLL, live, columns, slots, last, row_buf, restrict, table, acc, 0, CSLOT)
+    copy.wait()
+    applied = [
+        jnp.dot(row_buf[k], table[columns[last, k]], preferred_element_type=f32).astype(bf16) for k in range(slot_count)
+    ]
+    products = [jnp.dot(restrict, x, preferred_element_type=f32) for x in applied]
+    for k in range(slot_count):
+        acc[jnp.where(k < live, slots[last, k], CSLOT)] += products[k]
     out[...] = acc[0:CSLOT].astype(bf16)
 
 
-def main_kernel(columns, counts, aggregate, slots, stiffness, own, table, out, first_row, stiff, acc, stage, sems, out_sem):
+def main_kernel(listed, stiffness, own, table, out, first_row, stiff, restrict, acc, stage, sems, out_sem):
     rows, slot_count = stiffness.shape[:2]
-    last = rows - 1
-    for i in range(last):
-        pltpu.make_async_copy(stiffness.at[i], stiff.at[i], sems.at[i]).start()
+    for i in range(rows - 1):
+        pltpu.make_async_copy(stiffness.at[i], stiff.at[pl.ds(i * slot_count, slot_count)], sems.at[i]).start()
     acc[...] = jnp.zeros_like(acc)
-
-    @pl.loop(0, last)
-    def _(i):
-        pltpu.make_async_copy(stiffness.at[i], stiff.at[i], sems.at[i]).wait()
-        live = counts[0, i]
-        restrict = own[i].T
-        offset = aggregate[i] * CSLOT
-
-        @pl.loop(0, (live + (UNROLL - 1)) // UNROLL)
-        def _(c):
-            entries(c * UNROLL, UNROLL, live, columns, slots, i, stiff.at[i], restrict, table, acc,
-                    offset, NC_DEV * CSLOT)
-
+    for i in range(rows):
+        restrict[i] = own[i].T
+
+    def chunk(c, arrived):
+        words = [listed[c * UNROLL + u] for u in range(UNROLL)]
+        blocks = [w & (2**COLUMN_BIT - 1) for w in words]
+        needed = blocks[UNROLL - 1] // slot_count + 1
+        needed = jnp.where(c == chunks - 1, rows - 1, needed)
+
+        @pl.loop(arrived, needed)
+        def _(i):
+            pltpu.make_async_copy(stiffness.at[i], stiff.at[pl.ds(i * slot_count, slot_count)], sems.at[i]).wait()
+
+        applied = [
+            jnp.dot(stiff[b], table[(w >> COLUMN_BIT) & (2 ** (SEG_BIT - COLUMN_BIT) - 1)],
+                    preferred_element_type=f32).astype(bf16) for w, b in zip(words, blocks)
+        ]
+        products = [jnp.dot(restrict[b // slot_count], x, preferred_element_type=f32) for b, x in zip(blocks, applied)]
+        for w, z in zip(words, products):
+            acc[w >> SEG_BIT] += z
+        return jnp.maximum(arrived, needed)
+
+    chunks = (rows * AVGNZ) // UNROLL
+    lax.fori_loop(0, chunks, chunk, 0)
     first_row[...] = acc[0:CSLOT]
     for c in range(1, NC_DEV):
         stage[c - 1] = acc[c * CSLOT : (c + 1) * CSLOT].astype(bf16)
@@ -160,6 +184,8 @@
     g_own, g_other = as_blocks(g_own), as_blocks(g_other)
     n_ext = rows + n_dom * q
     limit = pltpu.CompilerParams(vmem_limit_bytes=40 * 2**20)
+    columns, counts, aggregate, coarse_slots, requests, stiffness = map(
+        in_hbm, (columns, counts, aggregate, coarse_slots, requests, stiffness))
     table, spill = pl.pallas_call(
         functools.partial(spill_kernel, n_dom, q),
         out_shape=(VMEM((n_ext, width, 2 * coarse), bf16), VMEM((CSLOT, dofs, 2 * coarse), bf16)),
@@ -171,19 +197,26 @@
         cost_estimate=pl.CostEstimate(flops=10**7, bytes_accessed=10**6, transcendentals=0),
     )(columns, counts, coarse_slots, requests, stiffness, in_vmem(own), in_vmem(other), in_vmem(g_own), in_vmem(g_other))
     incoming = lax.ppermute(spill, "blk", shift_pairs(lax.axis_size("blk"), 1))
+    listed = pl.pallas_call(
+        list_kernel,
+        out_shape=jax.ShapeDtypeStruct((rows * AVGNZ + 2 * slot_count,), jnp.int32),
+        in_specs=[spec(VMEM), spec(SMEM), spec(SMEM), spec(VMEM)],
+        out_specs=spec(SMEM),
+        scratch_shapes=[VMEM((rows, 128), jnp.int32), SMEM((rows, 128), jnp.int32), pltpu.SemaphoreType.DMA(())],
+    )(columns, counts, aggregate, coarse_slots)
     out_shape = jax.ShapeDtypeStruct((NC_DEV, CSLOT, coarse, 2 * coarse), bf16)
     out, partial = pl.pallas_call(
         main_kernel,
         out_shape=(out_shape, VMEM((CSLOT, coarse, 2 * coarse), f32)),
-        in_specs=[spec(SMEM)] * 4 + [spec(pl.ANY)] + [spec(VMEM)] * 2,
+        in_specs=[spec(SMEM), spec(pl.ANY)] + [spec(VMEM)] * 2,
         out_specs=(spec(pl.ANY), spec(VMEM)),
-        scratch_shapes=[VMEM((rows, slot_count, dofs, width), bf16),
+        scratch_shapes=[VMEM((rows * slot_count, dofs, width), bf16), VMEM((rows, coarse, dofs), bf16),
                         VMEM((NC_DEV * CSLOT + 1, coarse, 2 * coarse), f32),
                         VMEM((NC_DEV - 1, CSLOT, coarse, 2 * coarse), bf16),
                         pltpu.SemaphoreType.DMA((rows,)), pltpu.SemaphoreType.DMA(())],
         compiler_params=limit,
         cost_estimate=pl.CostEstimate(flops=10**9, bytes_accessed=10**7, transcendentals=0),
-    )(columns, counts, aggregate, coarse_slots, stiffness, in_vmem(own), in_vmem(table))
+    )(listed, stiffness, in_vmem(own), in_vmem(table))
     return pl.pallas_call(
         final_kernel,
         out_shape=out_shape,

time: 38.4 us -> 26.5 us (0.69)
  Pallas kernels: 22.1 us -> 15.5 us
  local copies, waits for them, and re-layouts: 7.36 us -> 2.29 us
    pallas_call x1, Pallas kernels: 17.7 us -> 8.45 us  [shards(): pl.pallas_call(main_kernel, out_shape=(out_shape, VMEM((CSLOT, coarse, 2...]
    unnamed x18 -> x2, local copies, waits for them, and re-layouts: 5.75 us -> 0.68 us
    pallas_call x0 -> x1, Pallas kernels: none -> 2.51 us  [shards(): pl.pallas_call(list_kernel, out_shape=jax.ShapeDtypeStruct((rows * AVGNZ...]
  transfers between devices with their start and end apart: 4 -> 4, of which waited for: 2 -> 2; matrix products, arithmetic and copies ran while one was open for 4% -> 5% of each run, Pallas kernels for 50% -> 46%
where the time goes in v2:
time: 26.5 us; the launch traced here: 26.1 us
  Pallas kernels  15.5 us (58%)
  starting transfers between devices  7.02 us (26%)
  local copies, waits for them, and re-layouts  2.29 us (9%)
  waiting for transfers between devices  1.23 us (5%)
    pallas_call x1, Pallas kernels, shards(): pl.pallas_call(main_kernel, out_shape=(out_shape, VMEM((CSLOT, coarse, 2...  8.45 us
    ppermute x1, starting transfers between devices, shards(): incoming = lax.ppermute(spill, 'blk', shift_pairs(lax.axis_size('blk'), 1))  3.6 us
    pallas_call x1, Pallas kernels, shards(): pl.pallas_call(functools.partial(spill_kernel, n_dom, q), out_shape=(VMEM...  2.61 us
    pallas_call x1, Pallas kernels, shards(): pl.pallas_call(list_kernel, out_shape=jax.ShapeDtypeStruct((rows * AVGNZ...  2.51 us
    ppermute x1, starting transfers between devices, shards(): other_flat = lax.ppermute(own_flat, 'field', [(0, 1), (1, 0)])  2.04 us
    ppermute x1, starting transfers between devices, shards(): g_other.append(lax.ppermute(part, ('dom', 'field'), pairs))  1.28 us
    another operation x1, local copies, waits for them, and re-layouts, shards(): as_blocks = lambda x: x.reshape(x.shape[0], dofs, coarse)  1.18 us
    ppermute x1, waiting for transfers between devices, shards(): g_other.append(lax.ppermute(part, ('dom', 'field'), pairs))  1.16 us
  transfers between devices with their start and end apart: 4, of which 2 were waited for; matrix products, arithmetic and copies ran while one was open for 5% of the time, Pallas kernels for 46%

profile of v2, /device:TPU:1, one launch (start us, length us, event | category | flops | bytes accessed | tf_op | source)
XLA Modules:
  0.0 26.1 jit_solution(16149493504722519535)
XLA Ops:
  0.0 2.0 %collective-permute-start = (bf16[16,4096]{1,0:T(8,128)(2,1)}, bf16[16,4096]{1,0:T(8,128)(2,1)S(1)}, u32[]{:S(2)}, u32[]{:S(2)}) collective-permute-start(bf16[16,4096]{1,0:T(8,128)(2,1)} %bitcast.3), channel_id=1, source_target_pairs={{0,1},{1,0},{2,3},{3,2},{4,5},{5,4},{6,7},{7,6},{8,9},{9,8},{10,11... | collective-permute-start | bytes 393224 | tf_op jit(solution)/shard_map/ppermute | solution.py:172
  2.0 1.1 %shard_map.74 = bf16[2,4096]{1,0:T(2,128)(2,1)S(1)} custom-call(s32[1,2,2]{2,1,0:T(2,128)} %requests.3, bf16[16,4096]{1,0:T(8,128)(2,1)} %bitcast.4), custom_call_target="tpu_custom_call" | custom-call | tf_op jit(solution)/shard_map/pallas_call | solution.py:53
  3.2 1.3 %collective-permute-start.2 = (bf16[2,4096]{1,0:T(2,128)(2,1)S(1)}, bf16[2,4096]{1,0:T(2,128)(2,1)S(1)}, u32[]{:S(2)}, u32[]{:S(2)}) collective-permute-start(bf16[2,4096]{1,0:T(2,128)(2,1)S(1)} %shard_map.74), channel_id=1, source_target_pairs={{0,17},{1,16},{16,1},{17,0},{2,19},{3,18},{18,3},{19,2},{4,21},{5,... | collective-permute-start | bytes 49160 | tf_op jit(solution)/shard_map/ppermute | solution.py:179
  4.4 0.1 collective-permute-start.1
  4.5 1.2 %reshape_squeeze.3.own = bf16[16,64,64]{2,1,0:T(8,128)(2,1)S(1)} reshape(bf16[16,1,4096]{2,0,1:T(8,128)(2,1)} %param.8) | data formatting | bytes 262144 | tf_op jit(solution)/shard_map/reshape;squeeze | solution.py:182
  5.7 1.2 %collective-permute-done.2 = bf16[2,4096]{1,0:T(2,128)(2,1)S(1)} collective-permute-done((bf16[2,4096]{1,0:T(2,128)(2,1)S(1)}, bf16[2,4096]{1,0:T(2,128)(2,1)S(1)}, u32[]{:S(2)}, u32[]{:S(2)}) %collective-permute-start.2) | collective-permute-done | bytes 16416 | tf_op jit(solution)/shard_map/ppermute | solution.py:179
  6.9 0.1 reshape.11.g_other
  7.0 0.1 collective-permute-done.1
  7.0 0.1 reshape.10.g_own
  7.1 0.0 collective-permute-done
  7.2 0.2 reshape.9.other
  7.4 2.6 %shard_map.75 = (bf16[20,128,128]{2,1,0:T(8,128)(2,1)S(1)}, bf16[27,64,128]{2,1,0:T(8,128)(2,1)S(1)}) custom-call(s32[16,27]{1,0:T(8,128)} %columns.3, s32[1,16]{1,0:T(1,128)} %counts.3, s32[16,27]{1,0:T(8,128)} %slots.3, s32[1,2,2]{2,1,0:T(2,128)} %requests.3, bf16[16,27,64,128]{3,2,1,0:T(8,128)(2,1)} %stiffness.3, ...), custom_call_target="tpu_custom_call" | custom-call | flops 10000000 | bytes 1000000 | tf_op jit(solution)/shard_map/pallas_call | solution.py:189
  10.0 3.6 %collective-permute-start.3 = (bf16[27,64,128]{2,1,0:T(8,128)(2,1)S(1)}, bf16[27,64,128]{2,1,0:T(8,128)(2,1)S(1)}, u32[]{:S(2)}, u32[]{:S(2)}) collective-permute-start(bf16[27,64,128]{2,1,0:T(8,128)(2,1)S(1)} %get-tuple-element.11), channel_id=1, source_target_pairs={{0,2},{2,4},{4,6},{6,8},{8,10},{10,12},{12,14},{14,0},{1,3},{3,5},... | collective-permute-start | bytes 1327112 | tf_op jit(solution)/shard_map/ppermute | solution.py:199
  13.6 2.5 %shard_map.73.listed = s32[310]{0:T(512)} custom-call(s32[16,27]{1,0:T(8,128)} %columns.3, s32[1,16]{1,0:T(1,128)} %counts.3, s32[16]{0:T(128)} %aggregate.1, s32[16,27]{1,0:T(8,128)} %slots.3), custom_call_target="tpu_custom_call" | custom-call | tf_op jit(solution)/shard_map/pallas_call | solution.py:200
  16.1 0.0 copy-start
  16.2 0.7 %copy-done = s32[310]{0:T(512)S(1)} copy-done((s32[310]{0:T(512)S(1)}, s32[310]{0:T(512)}, u32[]{:S(2)}) %copy-start) | copy-done | bytes 1264
  16.8 8.5 %shard_map.76 = (bf16[4,27,64,128]{3,2,1,0:T(8,128)(2,1)}, f32[27,64,128]{2,1,0:T(8,128)S(1)}) custom-call(s32[310]{0:T(512)S(1)} %copy-done, bf16[16,27,64,128]{3,2,1,0:T(8,128)(2,1)} %stiffness.3, bf16[16,64,64]{2,1,0:T(8,128)(2,1)S(1)} %reshape_squeeze.3.own, bf16[20,128,128]{2,1,0:T(8,128)(2,1)S(1)} %get-tuple-element.9.table), custom_call_target="tpu_custom_call" | custom-call | flops 1000000000 | bytes 10000000 | tf_op jit(solution)/shard_map/pallas_call | solution.py:208
  25.3 0.0 collective-permute-done.3.incoming
  25.3 0.8 %shard_map.77 = bf16[4,27,64,128]{3,2,1,0:T(8,128)(2,1)} custom-call(f32[27,64,128]{2,1,0:T(8,128)S(1)} %get-tuple-element.10.partial, bf16[27,64,128]{2,1,0:T(8,128)(2,1)S(1)} %collective-permute-done.3.incoming, bf16[4,27,64,128]{3,2,1,0:T(8,128)(2,1)} %get-tuple-element.12._), custom_call_target="tpu_custom_call", output_to_operand_aliasing={{}: (2, {})} | custom-call | tf_op jit(solution)/shard_map/pallas_call | solution.py:220
Async XLA Ops:
  0.0 7.1 %collective-permute-start = (bf16[16,4096]{1,0:T(8,128)(2,1)}, bf16[16,4096]{1,0:T(8,128)(2,1)S(1)}, u32[]{:S(2)}, u32[]{:S(2)}) collective-permute-start(bf16[16,4096]{1,0:T(8,128)(2,1)} %bitcast.3), channel_id=1, source_target_pairs={{0,1},{1,0},{2,3},{3,2},{4,5},{5,4},{6,7},{7,6},{8,9},{9,8},{10,11... | collective-permute-start | bytes 393224 | tf_op jit(solution)/shard_map/ppermute | solution.py:172
  3.2 3.7 %collective-permute-start.2 = (bf16[2,4096]{1,0:T(2,128)(2,1)S(1)}, bf16[2,4096]{1,0:T(2,128)(2,1)S(1)}, u32[]{:S(2)}, u32[]{:S(2)}) collective-permute-start(bf16[2,4096]{1,0:T(2,128)(2,1)S(1)} %shard_map.74), channel_id=1, source_target_pairs={{0,17},{1,16},{16,1},{17,0},{2,19},{3,18},{18,3},{19,2},{4,21},{5,... | collective-permute-start | bytes 49160 | tf_op jit(solution)/shard_map/ppermute | solution.py:179
  4.4 2.6 %collective-permute-start.1 = (bf16[2,4096]{1,0:T(2,128)(2,1)S(1)}, bf16[2,4096]{1,0:T(2,128)(2,1)S(1)}, u32[]{:S(2)}, u32[]{:S(2)}) collective-permute-start(bf16[2,4096]{1,0:T(2,128)(2,1)S(1)} %shard_map.74), channel_id=1, source_target_pairs={{0,16},{16,0},{1,17},{17,1},{2,18},{18,2},{3,19},{19,3},{4,20},{20... | collective-permute-start | bytes 49160 | tf_op jit(solution)/shard_map/ppermute | solution.py:177
  10.0 15.3 %collective-permute-start.3 = (bf16[27,64,128]{2,1,0:T(8,128)(2,1)S(1)}, bf16[27,64,128]{2,1,0:T(8,128)(2,1)S(1)}, u32[]{:S(2)}, u32[]{:S(2)}) collective-permute-start(bf16[27,64,128]{2,1,0:T(8,128)(2,1)S(1)} %get-tuple-element.11), channel_id=1, source_target_pairs={{0,2},{2,4},{4,6},{6,8},{8,10},{10,12},{12,14},{14,0},{1,3},{3,5},... | collective-permute-start | bytes 1327112 | tf_op jit(solution)/shard_map/ppermute | solution.py:199
  16.1 0.7 %copy-start = (s32[310]{0:T(512)S(1)}, s32[310]{0:T(512)}, u32[]{:S(2)}) copy-start(s32[310]{0:T(512)} %shard_map.73.listed) | copy-start | bytes 3724

commit v3 on v2

v3 whole, which is shorter than its diff:
```python
import functools

import jax
import jax.numpy as jnp
from jax import lax
from jax.experimental import pallas as pl
from jax.experimental.pallas import tpu as pltpu
from jax.sharding import PartitionSpec as P

CSLOT = 27
NC_DEV = 4
AVGNZ = 16
UNROLL = 32
COLUMN_BIT = 10
SEG_BIT = 16

VMEM = pltpu.VMEM
SMEM = pltpu.SMEM
f32 = jnp.float32
bf16 = jnp.bfloat16


def in_vmem(x):
    return pltpu.with_memory_space_constraint(x, VMEM)


def in_hbm(x):
    return pltpu.with_memory_space_constraint(x, pltpu.HBM)


def spec(space):
    return pl.BlockSpec(memory_space=space)


def shift_pairs(n, by):
    return [(i, (i + by) % n) for i in range(n)]


def prepare_kernel(n_dom, q, requests, flat, columns, slots, counts, aggregate, requests_v, picked, copied, words):
    me = lax.axis_index("dom")
    rows, slot_count = columns.shape
    lane = lax.broadcasted_iota(jnp.int32, (1, rows), 1)
    hot = []
    for s in range(1, n_dom):
        to = lax.rem(me + s, n_dom)
        for r in range(q):
            hot.append((lane == requests[0, to, r]).astype(f32))
    hot = jnp.concatenate(hot, axis=0).astype(bf16)
    own = flat[...]
    picked[...] = jnp.dot(hot, own, preferred_element_type=f32).astype(bf16)
    copied[...] = own
    block = lax.broadcasted_iota(jnp.int32, (rows, slot_count), 0) * slot_count
    block = block + lax.broadcasted_iota(jnp.int32, (rows, slot_count), 1)
    words[0:rows, 0:slot_count] = block + (columns[...] << COLUMN_BIT) + (slots[...] << SEG_BIT)
    words[rows : rows + 1, 0:rows] = counts[...]
    words[rows + 1 : rows + 2, 0:rows] = aggregate[...]
    words[rows + 2 : rows + 2 + n_dom, 0:q] = requests_v[0]


def table_of(n_dom, q, words, own, other, g_own, g_other, table):
    rows, dofs = own.shape[:2]
    first = lax.axis_index("field") == 0
    me = lax.axis_index("dom")

    def put(j, mine, theirs):
        zero = jnp.zeros((dofs, dofs), bf16)
        top = jnp.where(first, mine, theirs)
        bottom = jnp.where(first, theirs, mine)
        table[j] = jnp.concatenate(
            [jnp.concatenate([top, zero], axis=1), jnp.concatenate([zero, bottom], axis=1)], axis=0)

    for j in range(rows):
        put(j, own[j], other[j])
    for s in range(1, n_dom):
        source = lax.rem(me + n_dom - s, n_dom)
        for r in range(q):
            put(rows + source * q + r, g_own[(s - 1) * q + r], g_other[(s - 1) * q + r])
    for r in range(q):
        table[rows + me * q + r] = table[words[rows + 2 + me, r]]


def block_of(word):
    return word & (2**COLUMN_BIT - 1)


def column_of(word):
    return (word >> COLUMN_BIT) & (2 ** (SEG_BIT - COLUMN_BIT) - 1)


def spill_kernel(n_dom, q, words, stiffness, own, other, g_own, g_other, table, out, row_buf, acc, sem):
    rows, slot_count = stiffness.shape[:2]
    last = rows - 1
    copy = pltpu.make_async_copy(stiffness.at[last], row_buf, sem)
    copy.start()
    table_of(n_dom, q, words, own, other, g_own, g_other, table)
    acc[...] = jnp.zeros_like(acc)
    live = words[rows, last]
    restrict = own[last].T
    copy.wait()
    listed = [words[last, k] for k in range(slot_count)]
    applied = [
        jnp.dot(row_buf[k], table[column_of(listed[k])], preferred_element_type=f32).astype(bf16)
        for k in range(slot_count)
    ]
    products = [jnp.dot(restrict, x, preferred_element_type=f32) for x in applied]
    for k in range(slot_count):
        acc[jnp.where(k < live, listed[k] >> SEG_BIT, CSLOT)] += products[k]
    out[...] = acc[0:CSLOT].astype(bf16)


def main_kernel(words, stiffness, own, table, out, first_row, listed, stiff, restrict, acc, stage, sems, out_sems):
    rows, slot_count = stiffness.shape[:2]
    for i in range(rows - 1):
        pltpu.make_async_copy(stiffness.at[i], stiff.at[pl.ds(i * slot_count, slot_count)], sems.at[i]).start()
    acc[...] = jnp.zeros_like(acc)
    base = 0
    for i in range(rows - 1):
        offset = (words[rows + 1, i] * CSLOT) << SEG_BIT
        for k in range(slot_count):
            listed[base + k] = words[i, k] + offset
        base = base + words[rows, i]
    for k in range(slot_count):
        listed[base + k] = (NC_DEV * CSLOT) << SEG_BIT
    for i in range(rows):
        restrict[i] = own[i].T

    def chunk(c, arrived):
        taken = [listed[c * UNROLL + u] for u in range(UNROLL)]
        blocks = [block_of(w) for w in taken]
        needed = blocks[UNROLL - 1] // slot_count + 1
        needed = jnp.where(c == chunks - 1, rows - 1, needed)

        @pl.loop(arrived, needed)
        def _(i):
            pltpu.make_async_copy(stiffness.at[i], stiff.at[pl.ds(i * slot_count, slot_count)], sems.at[i]).wait()

        applied = [
            jnp.dot(stiff[b], table[column_of(w)], preferred_element_type=f32).astype(bf16)
            for w, b in zip(taken, blocks)
        ]
        products = [jnp.dot(restrict[b // slot_count], x, preferred_element_type=f32) for b, x in zip(blocks, applied)]
        for w, z in zip(taken, products):
            acc[w >> SEG_BIT] += z
        return jnp.maximum(arrived, needed)

    chunks = (rows * AVGNZ) // UNROLL
    lax.fori_loop(0, chunks, chunk, 0)
    copies = [pltpu.make_async_copy(stage.at[c - 1], out.at[c], out_sems.at[c - 1]) for c in range(1, NC_DEV)]
    for c in range(1, NC_DEV):
        stage[c - 1] = acc[c * CSLOT : (c + 1) * CSLOT].astype(bf16)
        copies[c - 1].start()
    first_row[...] = acc[0:CSLOT]
    for copy in copies:
        copy.wait()


def final_kernel(partial, incoming, _, out, stage, sems):
    parts = sems.shape[0]
    size = CSLOT // parts
    copies = [pltpu.make_async_copy(stage.at[pl.ds(p * size, size)], out.at[0, pl.ds(p * size, size)], sems.at[p])
              for p in range(parts)]
    for p in range(parts):
        part = pl.ds(p * size, size)
        stage[part] = (partial[part] + incoming[part].astype(f32)).astype(bf16)
        copies[p].start()
    for copy in copies:
        copy.wait()


def shards(stiffness, prolong, columns, counts, aggregate, coarse_slots, requests):
    rows, slot_count, dofs, width = stiffness.shape
    coarse = prolong.shape[2] // dofs
    n_dom = lax.axis_size("dom")
    n_field = lax.axis_size("field")
    q = requests.shape[2]
    n_ext = rows + n_dom * q
    block_shape = (coarse, 2 * coarse)
    limit = pltpu.CompilerParams(vmem_limit_bytes=40 * 2**20)
    own_flat = prolong[:, 0, :]
    other_flat = lax.ppermute(own_flat, "field", [(0, 1), (1, 0)])
    stiffness = in_hbm(stiffness)
    picked, own_copy, words = pl.pallas_call(
        functools.partial(prepare_kernel, n_dom, q),
        out_shape=(VMEM(((n_dom - 1) * q, own_flat.shape[1]), bf16), VMEM(own_flat.shape, bf16),
                   VMEM((-(-(rows + 2 + n_dom) // 8) * 8, 128), jnp.int32)),
        in_specs=[spec(SMEM)] + [spec(VMEM)] * 6,
        out_specs=(spec(VMEM),) * 3,
    )(*map(in_hbm, (requests, own_flat, columns, coarse_slots, counts, aggregate[None], requests)))
    g_own, g_other = [], []
    for s in range(1, n_dom):
        part = picked[(s - 1) * q : s * q]
        g_own.append(lax.ppermute(part, "dom", shift_pairs(n_dom, s)))
        pairs = [(d * n_field + f, ((d + s) % n_dom) * n_field + 1 - f) for d in range(n_dom) for f in range(n_field)]
        g_other.append(lax.ppermute(part, ("dom", "field"), pairs))
    g_own = jnp.concatenate(g_own, axis=0)
    g_other = jnp.concatenate(g_other, axis=0)
    as_blocks = lambda x: in_vmem(x.reshape(x.shape[0], dofs, coarse))
    own, other = as_blocks(own_copy), as_blocks(other_flat)
    g_own, g_other = as_blocks(g_own), as_blocks(g_other)
    words = in_vmem(words)
    table, spill = pl.pallas_call(
        functools.partial(spill_kernel, n_dom, q),
        out_shape=(VMEM((n_ext, width, 2 * coarse), bf16), VMEM((CSLOT, *block_shape), bf16)),
        in_specs=[spec(SMEM), spec(pl.ANY)] + [spec(VMEM)] * 4,
        out_specs=(spec(VMEM), spec(VMEM)),
        scratch_shapes=[VMEM((slot_count, dofs, width), bf16), VMEM((CSLOT + 1, *block_shape), f32),
                        pltpu.SemaphoreType.DMA(())],
        compiler_params=limit,
        cost_estimate=pl.CostEstimate(flops=10**7, bytes_accessed=10**6, transcendentals=0),
    )(words, stiffness, own, other, g_own, g_other)
    incoming = lax.ppermute(spill, "blk", shift_pairs(lax.axis_size("blk"), 1))
    out_shape = jax.ShapeDtypeStruct((NC_DEV, CSLOT, *block_shape), bf16)
    out, partial = pl.pallas_call(
        main_kernel,
        out_shape=(out_shape, VMEM((CSLOT, *block_shape), f32)),
        in_specs=[spec(SMEM), spec(pl.ANY)] + [spec(VMEM)] * 2,
        out_specs=(spec(pl.ANY), spec(VMEM)),
        scratch_shapes=[SMEM((rows * AVGNZ + 2 * slot_count,), jnp.int32),
                        VMEM((rows * slot_count, dofs, width), bf16), VMEM((rows, coarse, dofs), bf16),
                        VMEM((NC_DEV * CSLOT + 1, *block_shape), f32),
                        VMEM((NC_DEV - 1, CSLOT, *block_shape), bf16),
                        pltpu.SemaphoreType.DMA((rows,)), pltpu.SemaphoreType.DMA((NC_DEV - 1,))],
        compiler_params=limit,
        cost_estimate=pl.CostEstimate(flops=10**9, bytes_accessed=10**7, transcendentals=0),
    )(words, stiffness, own, in_vmem(table))
    return pl.pallas_call(
        final_kernel,
        out_shape=out_shape,
        in_specs=[spec(VMEM), spec(VMEM), spec(pl.ANY)],
        out_specs=spec(pl.ANY),
        scratch_shapes=[VMEM((CSLOT, *block_shape), bf16), pltpu.SemaphoreType.DMA((3,))],
        input_output_aliases={2: 0},
        compiler_params=limit,
    )(in_vmem(partial), in_vmem(incoming), out)


def solution(mesh):
    in_specs = (
        P(("dom", "blk"), None, "field", None),
        P(("dom", "blk"), "field", None),
        P(("dom", "blk"), None),
        P(("dom", "blk"), None),
        P(("dom", "blk")),
        P(("dom", "blk"), None),
        P(("dom", "blk"), None, None),
    )
    out_specs = P(("dom", "blk"), None, "field", None)
    return jax.shard_map(shards, mesh=mesh, in_specs=in_specs, out_specs=out_specs, check_vma=False)
```

time: 26.5 us -> 23.1 us (0.87)
  Pallas kernels: 15.5 us -> 13 us
  local copies, waits for them, and re-layouts: 2.29 us -> 0.67 us
  waiting for transfers between devices: 1.23 us -> 2.16 us
    pallas_call x3 -> x2, Pallas kernels: 12.1 us -> 9.82 us  [the longest x1 8.69 us: shards(): pl.pallas_call(main_kernel, out_shape=(out_shape, VMEM((CSLOT, *block_sha...]
    another operation x1 -> x0, local copies, waits for them, and re-layouts: 1.18 us -> none  [shards(): as_blocks = lambda x: x.reshape(x.shape[0], dofs, coarse)]
    ppermute x1, waiting for transfers between devices: 1.16 us -> 2.09 us  [shards(): g_other.append(lax.ppermute(part, ('dom', 'field'), pairs))]
    unnamed x2 -> x0, local copies, waits for them, and re-layouts: 0.68 us -> none
    reshape x3 -> x4, local copies, waits for them, and re-layouts: 0.43 us -> 0.67 us  [shards(): as_blocks = lambda x: in_vmem(x.reshape(x.shape[0], dofs, coarse))]
  transfers between devices with their start and end apart: 4 -> 4, of which waited for: 2 -> 2; matrix products, arithmetic and copies ran while one was open for 5% -> 2% of each run, Pallas kernels for 46% -> 43%
where the time goes in v3:
time: 23.1 us; the launch traced here: 22.9 us
  Pallas kernels  13 us (56%)
  starting transfers between devices  7.04 us (30%)
  waiting for transfers between devices  2.16 us (9%)
  local copies, waits for them, and re-layouts  0.67 us (3%)
    pallas_call x1, Pallas kernels, shards(): pl.pallas_call(main_kernel, out_shape=(out_shape, VMEM((CSLOT, *block_sha...  8.69 us
    ppermute x1, starting transfers between devices, shards(): incoming = lax.ppermute(spill, 'blk', shift_pairs(lax.axis_size('blk'), 1))  3.62 us
    pallas_call x1, Pallas kernels, shards(): pl.pallas_call(functools.partial(spill_kernel, n_dom, q), out_shape=(VMEM...  2.37 us
    ppermute x1, waiting for transfers between devices, shards(): g_other.append(lax.ppermute(part, ('dom', 'field'), pairs))  2.09 us
    ppermute x1, starting transfers between devices, shards(): other_flat = lax.ppermute(own_flat, 'field', [(0, 1), (1, 0)])  2.04 us
    ppermute x1, starting transfers between devices, shards(): g_other.append(lax.ppermute(part, ('dom', 'field'), pairs))  1.27 us
    pallas_call x1, Pallas kernels, shards(): pl.pallas_call(functools.partial(prepare_kernel, n_dom, q), out_shape=(VM...  1.12 us
    pallas_call x1, Pallas kernels, shards(): pl.pallas_call(final_kernel, out_shape=out_shape, in_specs=[spec(VMEM), s...  0.82 us
  transfers between devices with their start and end apart: 4, of which 2 were waited for; matrix products, arithmetic and copies ran while one was open for 2% of the time, Pallas kernels for 43%

profile of v3, /device:TPU:1, one launch (start us, length us, event | category | flops | bytes accessed | tf_op | source)
XLA Modules:
  0.0 22.9 jit_solution(14442683048295845581)
XLA Ops:
  0.0 2.0 %collective-permute-start = (bf16[16,4096]{1,0:T(8,128)(2,1)}, bf16[16,4096]{1,0:T(8,128)(2,1)S(1)}, u32[]{:S(2)}, u32[]{:S(2)}) collective-permute-start(bf16[16,4096]{1,0:T(8,128)(2,1)} %bitcast.2), channel_id=1, source_target_pairs={{0,1},{1,0},{2,3},{3,2},{4,5},{5,4},{6,7},{7,6},{8,9},{9,8},{10,11... | collective-permute-start | bytes 393224 | tf_op jit(solution)/shard_map/ppermute | solution.py:180
  2.0 1.1 %shard_map.73 = (bf16[2,4096]{1,0:T(2,128)(2,1)S(1)}, bf16[16,4096]{1,0:T(8,128)(2,1)S(1)}, s32[24,128]{1,0:T(8,128)S(1)}) custom-call(s32[1,2,2]{2,1,0:T(2,128)} %requests_v.1, bf16[16,4096]{1,0:T(8,128)(2,1)} %bitcast.3, s32[16,27]{1,0:T(8,128)} %columns.1, s32[16,27]{1,0:T(8,128)} %slots.1, s32[1,16]{1,0:T(1,128)} %counts.1, s32[1,16]{1,0:T(1,128)} %bitcast.4, ...), custom_call_target="tpu_custom_call" | custom-call | tf_op jit(solution)/shard_map/pallas_call | solution.py:182
  3.2 1.3 %collective-permute-start.2 = (bf16[2,4096]{1,0:T(2,128)(2,1)S(1)}, bf16[2,4096]{1,0:T(2,128)(2,1)S(1)}, u32[]{:S(2)}, u32[]{:S(2)}) collective-permute-start(bf16[2,4096]{1,0:T(2,128)(2,1)S(1)} %get-tuple-element.14), channel_id=1, source_target_pairs={{0,17},{1,16},{16,1},{17,0},{2,19},{3,18},{18,3},{19,2},{4,21},{5,... | collective-permute-start | bytes 49160 | tf_op jit(solution)/shard_map/ppermute | solution.py:194
  4.4 0.1 collective-permute-start.1
  4.6 0.2 %reshape.12.own = bf16[16,64,64]{2,1,0:T(8,128)(2,1)S(1)} reshape(bf16[16,4096]{1,0:T(8,128)(2,1)S(1)} %get-tuple-element.13) | data formatting | bytes 262144 | tf_op jit(solution)/shard_map/reshape | solution.py:197
  4.8 2.1 %collective-permute-done.2 = bf16[2,4096]{1,0:T(2,128)(2,1)S(1)} collective-permute-done((bf16[2,4096]{1,0:T(2,128)(2,1)S(1)}, bf16[2,4096]{1,0:T(2,128)(2,1)S(1)}, u32[]{:S(2)}, u32[]{:S(2)}) %collective-permute-start.2) | collective-permute-done | bytes 16416 | tf_op jit(solution)/shard_map/ppermute | solution.py:194
  6.9 0.1 reshape.15.g_other
  7.0 0.1 collective-permute-done.1
  7.1 0.1 reshape.14.g_own
  7.2 0.0 collective-permute-done
  7.2 0.2 %reshape.13.other = bf16[16,64,64]{2,1,0:T(8,128)(2,1)S(1)} reshape(bf16[16,4096]{1,0:T(8,128)(2,1)S(1)} %collective-permute-done) | data formatting | bytes 262144 | tf_op jit(solution)/shard_map/reshape | solution.py:197
  7.4 2.4 %shard_map.74 = (bf16[20,128,128]{2,1,0:T(8,128)(2,1)S(1)}, bf16[27,64,128]{2,1,0:T(8,128)(2,1)S(1)}) custom-call(s32[24,128]{1,0:T(8,128)S(1)} %get-tuple-element.12.words, bf16[16,27,64,128]{3,2,1,0:T(8,128)(2,1)} %stiffness.3, bf16[16,64,64]{2,1,0:T(8,128)(2,1)S(1)} %reshape.12.own, bf16[16,64,64]{2,1,0:T(8,128)(2,1)S(1)} %reshape.13.other, ...), custom_call_target="tpu_custom_call" | custom-call | flops 10000000 | bytes 1000000 | tf_op jit(solution)/shard_map/pallas_call | solution.py:201
  9.8 3.6 %collective-permute-start.3 = (bf16[27,64,128]{2,1,0:T(8,128)(2,1)S(1)}, bf16[27,64,128]{2,1,0:T(8,128)(2,1)S(1)}, u32[]{:S(2)}, u32[]{:S(2)}) collective-permute-start(bf16[27,64,128]{2,1,0:T(8,128)(2,1)S(1)} %get-tuple-element.17), channel_id=1, source_target_pairs={{0,2},{2,4},{4,6},{6,8},{8,10},{10,12},{12,14},{14,0},{1,3},{3,5},... | collective-permute-start | bytes 1327112 | tf_op jit(solution)/shard_map/ppermute | solution.py:211
  13.4 8.7 %shard_map.75 = (bf16[4,27,64,128]{3,2,1,0:T(8,128)(2,1)}, f32[27,64,128]{2,1,0:T(8,128)S(1)}) custom-call(s32[24,128]{1,0:T(8,128)S(1)} %get-tuple-element.12.words, bf16[16,27,64,128]{3,2,1,0:T(8,128)(2,1)} %stiffness.3, bf16[16,64,64]{2,1,0:T(8,128)(2,1)S(1)} %reshape.12.own, bf16[20,128,128]{2,1,0:T(8,128)(2,1)S(1)} %get-tuple-element.15.table), custom_call_target="tpu_custom_call" | custom-call | flops 1000000000 | bytes 10000000 | tf_op jit(solution)/shard_map/pallas_call | solution.py:213
  22.1 0.0 collective-permute-done.3.incoming
  22.1 0.8 %shard_map.76 = bf16[4,27,64,128]{3,2,1,0:T(8,128)(2,1)} custom-call(f32[27,64,128]{2,1,0:T(8,128)S(1)} %get-tuple-element.16.partial, bf16[27,64,128]{2,1,0:T(8,128)(2,1)S(1)} %collective-permute-done.3.incoming, bf16[4,27,64,128]{3,2,1,0:T(8,128)(2,1)} %get-tuple-element.18._), custom_call_target="tpu_custom_call", output_to_operand_aliasing={{}: (2, {})} | custom-call | tf_op jit(solution)/shard_map/pallas_call | solution.py:226
Async XLA Ops:
  0.0 7.2 %collective-permute-start = (bf16[16,4096]{1,0:T(8,128)(2,1)}, bf16[16,4096]{1,0:T(8,128)(2,1)S(1)}, u32[]{:S(2)}, u32[]{:S(2)}) collective-permute-start(bf16[16,4096]{1,0:T(8,128)(2,1)} %bitcast.2), channel_id=1, source_target_pairs={{0,1},{1,0},{2,3},{3,2},{4,5},{5,4},{6,7},{7,6},{8,9},{9,8},{10,11... | collective-permute-start | bytes 393224 | tf_op jit(solution)/shard_map/ppermute | solution.py:180
  3.2 3.7 %collective-permute-start.2 = (bf16[2,4096]{1,0:T(2,128)(2,1)S(1)}, bf16[2,4096]{1,0:T(2,128)(2,1)S(1)}, u32[]{:S(2)}, u32[]{:S(2)}) collective-permute-start(bf16[2,4096]{1,0:T(2,128)(2,1)S(1)} %get-tuple-element.14), channel_id=1, source_target_pairs={{0,17},{1,16},{16,1},{17,0},{2,19},{3,18},{18,3},{19,2},{4,21},{5,... | collective-permute-start | bytes 49160 | tf_op jit(solution)/shard_map/ppermute | solution.py:194
  4.4 2.6 %collective-permute-start.1 = (bf16[2,4096]{1,0:T(2,128)(2,1)S(1)}, bf16[2,4096]{1,0:T(2,128)(2,1)S(1)}, u32[]{:S(2)}, u32[]{:S(2)}) collective-permute-start(bf16[2,4096]{1,0:T(2,128)(2,1)S(1)} %get-tuple-element.14), channel_id=1, source_target_pairs={{0,16},{16,0},{1,17},{17,1},{2,18},{18,2},{3,19},{19,3},{4,20},{20... | collective-permute-start | bytes 49160 | tf_op jit(solution)/shard_map/ppermute | solution.py:192
  9.8 12.3 %collective-permute-start.3 = (bf16[27,64,128]{2,1,0:T(8,128)(2,1)S(1)}, bf16[27,64,128]{2,1,0:T(8,128)(2,1)S(1)}, u32[]{:S(2)}, u32[]{:S(2)}) collective-permute-start(bf16[27,64,128]{2,1,0:T(8,128)(2,1)S(1)} %get-tuple-element.17), channel_id=1, source_target_pairs={{0,2},{2,4},{4,6},{6,8},{8,10},{10,12},{12,14},{14,0},{1,3},{3,5},... | collective-permute-start | bytes 1327112 | tf_op jit(solution)/shard_map/ppermute | solution.py:211

commit v4 on v3

v4 whole, which is shorter than its diff:
```python
import functools

import jax
import jax.numpy as jnp
from jax import lax
from jax.experimental import pallas as pl
from jax.experimental.pallas import tpu as pltpu
from jax.sharding import PartitionSpec as P

CSLOT = 27
NC_DEV = 4
HALF = 14
AVGNZ = 16
UNROLL = 32
EARLY = 2
COLUMN_BIT = 10
SEG_BIT = 16
UNUSED = NC_DEV * CSLOT

VMEM = pltpu.VMEM
SMEM = pltpu.SMEM
f32 = jnp.float32
bf16 = jnp.bfloat16


def in_vmem(x):
    return pltpu.with_memory_space_constraint(x, VMEM)


def in_hbm(x):
    return pltpu.with_memory_space_constraint(x, pltpu.HBM)


def spec(space):
    return pl.BlockSpec(memory_space=space)


def shift_pairs(n, by):
    return [(i, (i + by) % n) for i in range(n)]


def prepare_kernel(n_dom, q, flat, columns, slots, counts, aggregate, requests, stiffness, picked, copied, words,
                   last_row, columns_v, slots_v, counts_v, aggregate_v, requests_v, sems):
    rows, slot_count = columns.shape
    pairs = ((flat, copied), (requests, requests_v), (columns, columns_v), (slots, slots_v), (counts, counts_v),
             (aggregate, aggregate_v), (stiffness.at[rows - 1], last_row))
    copies = [pltpu.make_async_copy(source, target, sems.at[i]) for i, (source, target) in enumerate(pairs)]
    for copy in copies:
        copy.start()
    me = lax.axis_index("dom")
    lane = lax.broadcasted_iota(jnp.int32, (1, rows), 1)
    block = lax.broadcasted_iota(jnp.int32, (rows, slot_count), 0) * slot_count
    block = block + lax.broadcasted_iota(jnp.int32, (rows, slot_count), 1)
    copies[0].wait()
    copies[1].wait()
    hot = []
    for s in range(1, n_dom):
        to = lax.rem(me + s, n_dom)
        asked = requests_v[0, pl.ds(to, 1), :]
        for r in range(q):
            hot.append((lane == asked[:, r : r + 1]).astype(f32))
    hot = jnp.concatenate(hot, axis=0).astype(bf16)
    picked[...] = jnp.dot(hot, copied[...], preferred_element_type=f32).astype(bf16)
    for copy in copies[2:6]:
        copy.wait()
    words[0:rows, 0:slot_count] = block + (columns_v[...] << COLUMN_BIT) + (slots_v[...] << SEG_BIT)
    words[rows : rows + 1, 0:rows] = counts_v[...]
    words[rows + 1 : rows + 2, 0:rows] = aggregate_v[...]
    words[rows + 2 : rows + 2 + n_dom, 0:q] = requests_v[0]
    copies[6].wait()


def block_of(word):
    return word & (2**COLUMN_BIT - 1)


def column_of(word):
    return (word >> COLUMN_BIT) & (2 ** (SEG_BIT - COLUMN_BIT) - 1)


def early_kernel(words_v, last_row, own, stiffness, words, restricted, restricted_early, row_buf, sem, sems):
    slot_count = last_row.shape[0]
    copy = pltpu.make_async_copy(words_v, words, sem)
    copy.start()
    rows = [pltpu.make_async_copy(stiffness.at[i], row_buf.at[i], sems.at[i]) for i in range(EARLY)]
    for row in rows:
        row.start()
    restrict = own[own.shape[0] - 1].T
    for k in range(slot_count):
        restricted[k] = jnp.dot(restrict, last_row[k], preferred_element_type=f32).astype(bf16)
    copy.wait()
    for i in range(EARLY):
        restrict = own[i].T
        rows[i].wait()
        for k in range(slot_count):
            y = jnp.dot(restrict, row_buf[i, k], preferred_element_type=f32)
            restricted_early[i * slot_count + k] = y.astype(bf16)


def unfold(flat, tiles, lines, dofs):
    count, size = flat.shape
    wide = flat[...].astype(f32)
    for t in range(size // 128):
        tiles[t * count : (t + 1) * count] = wide[:, t * 128 : (t + 1) * 128]
    blocks = []
    for r in range(count):
        pairs = tiles[pl.ds(r, dofs // 2, stride=count)]
        lines[pl.ds(0, dofs // 2, stride=2)] = pairs
        lines[pl.ds(1, dofs // 2, stride=2)] = pltpu.roll(pairs, 64, 1)
        blocks.append(lines[:, 0:64].astype(bf16))
    return blocks


def lane_half():
    return lax.broadcasted_iota(jnp.int32, (64, 128), 1) < 64


def corner(field, dofs, value):
    zero = jnp.zeros_like(value)
    left = jnp.concatenate([value, zero], axis=1)
    right = jnp.concatenate([zero, value], axis=1)
    return pl.multiple_of(field * dofs, dofs), jnp.where(field == 0, left, right)


def fill_table(n_dom, q, field, words, blocks, ghosts, table, tiles, lines):
    rows, dofs = blocks.shape[:2]
    me = lax.axis_index("dom")

    def put(j, value):
        start, lines = corner(field, dofs, value)
        table[j, pl.ds(start, dofs)] = lines

    for j in range(rows):
        put(j, blocks[j])
    ghosts = unfold(ghosts, tiles, lines, dofs)
    for s in range(1, n_dom):
        source = lax.rem(me + n_dom - s, n_dom)
        for r in range(q):
            put(rows + source * q + r, ghosts[(s - 1) * q + r])
    for r in range(q):
        put(rows + me * q + r, blocks[words[rows + 2 + me, r]])


def spill_half(rows, field, words, restricted, table, out, acc):
    slot_count = restricted.shape[0]
    last = rows - 1
    acc[...] = jnp.zeros_like(acc)
    live = words[rows, last]
    listed = [words[last, k] for k in range(slot_count)]
    products = [
        jnp.dot(restricted[k], table[column_of(listed[k])], preferred_element_type=f32) for k in range(slot_count)
    ]
    for k in range(slot_count):
        acc[jnp.where(k < live, listed[k] >> SEG_BIT, CSLOT)] += products[k]
    keep = lane_half() == (field == 0)
    for s in range(HALF):
        block = acc[s]
        if s + HALF < CSLOT:
            block = jnp.where(keep, block, pltpu.roll(acc[s + HALF], 64, 1))
        out[s] = block.astype(bf16)


def own_spill_kernel(n_dom, q, words, restricted, own, ghosts, table, out, acc, tiles, lines):
    field = lax.axis_index("field")
    table[...] = jnp.zeros_like(table)
    fill_table(n_dom, q, field, words, own, ghosts, table, tiles, lines)
    spill_half(own.shape[0], field, words, restricted, table, out, acc)


def other_spill_kernel(n_dom, q, words, restricted, other, ghosts, _, table, out, acc, tiles, lines):
    field = 1 - lax.axis_index("field")
    fill_table(n_dom, q, field, words, other, ghosts, table, tiles, lines)
    spill_half(other.shape[0], field, words, restricted, table, out, acc)


def fill_list(words, listed, rows, slot_count, lead):
    base = 0
    for i in range(rows - 1):
        if i == EARLY:
            for k in range(UNROLL):
                listed[base + k] = UNUSED << SEG_BIT
            first_length = base
            base = lead
        offset = (words[rows + 1, i] * CSLOT) << SEG_BIT
        for k in range(slot_count):
            listed[base + k] = words[i, k] + offset
        base = base + words[rows, i]
    for k in range(UNROLL):
        listed[base + k] = (UNUSED << SEG_BIT) + (rows - 2) * slot_count
    return first_length, base - lead


def main_kernel(lead, words, stiffness, own, restricted_early, table, later_rows, first_row, listed, stiff, restrict, acc,
                sems):
    rows, slot_count = stiffness.shape[:2]

    def row_copy(i):
        part = pl.ds((i - EARLY) * slot_count, slot_count)
        return pltpu.make_async_copy(stiffness.at[i], stiff.at[part], sems.at[i])

    for i in range(EARLY, rows - 1):
        row_copy(i).start()
    first_length, second_length = fill_list(words, listed, rows, slot_count, lead)
    for i in range(EARLY, rows - 1):
        restrict[i] = own[i].T
    acc[...] = jnp.zeros_like(acc)

    def add(taken, restricted):
        products = [jnp.dot(y, table[column_of(w)], preferred_element_type=f32) for w, y in zip(taken, restricted)]
        for w, z in zip(taken, products):
            acc[w >> SEG_BIT] += z

    @pl.loop(0, (first_length + UNROLL - 1) // UNROLL)
    def _(c):
        taken = [listed[c * UNROLL + u] for u in range(UNROLL)]
        add(taken, [restricted_early[block_of(w)] for w in taken])

    def chunk(c, arrived):
        taken = [listed[lead + c * UNROLL + u] for u in range(UNROLL)]
        blocks = [block_of(w) for w in taken]
        needed = blocks[UNROLL - 1] // slot_count + 1

        @pl.loop(arrived, needed)
        def _(i):
            row_copy(i).wait()

        add(taken, [
            jnp.dot(restrict[b // slot_count], stiff[b - EARLY * slot_count], preferred_element_type=f32).astype(bf16)
            for b in blocks
        ])
        return needed

    lax.fori_loop(0, (second_length + UNROLL - 1) // UNROLL, chunk, EARLY)
    for c in range(1, NC_DEV):
        later_rows[c - 1] = acc[c * CSLOT : (c + 1) * CSLOT].astype(bf16)
    first_row[...] = acc[0:CSLOT]


def final_kernel(partial, own_part, other_part, later_rows, out, stage, sems):
    keep = lane_half() == (lax.axis_index("field") == 0)
    later = [pltpu.make_async_copy(later_rows.at[c - 1], out.at[c], sems.at[c]) for c in range(1, NC_DEV)]
    for copy in later:
        copy.start()
    copies = [pltpu.make_async_copy(stage.at[pl.ds(s, n)], out.at[0, pl.ds(s, n)], sem)
              for s, n, sem in ((0, HALF, sems.at[0]), (HALF, CSLOT - HALF, sems.at[NC_DEV]))]
    for s in range(HALF):
        mine, theirs = own_part[s].astype(f32), other_part[s].astype(f32)
        stage[s] = (partial[s] + jnp.where(keep, mine, theirs)).astype(bf16)
    copies[0].start()
    for s in range(HALF, CSLOT):
        mine, theirs = own_part[s - HALF].astype(f32), other_part[s - HALF].astype(f32)
        stage[s] = (partial[s] + pltpu.roll(jnp.where(keep, theirs, mine), 64, 1)).astype(bf16)
    copies[1].start()
    for copy in later + copies:
        copy.wait()


def shards(stiffness, prolong, columns, counts, aggregate, coarse_slots, requests):
    rows, slot_count, dofs, width = stiffness.shape
    coarse = prolong.shape[2] // dofs
    n_dom = lax.axis_size("dom")
    n_field = lax.axis_size("field")
    q = requests.shape[2]
    n_ext = rows + n_dom * q
    limit = pltpu.CompilerParams(vmem_limit_bytes=24 * 2**20)
    own_flat = prolong[:, 0, :]
    other_flat = lax.ppermute(own_flat, "field", [(0, 1), (1, 0)])
    n_words = -(-(rows + 2 + n_dom) // 8) * 8
    integers = lambda *shape: VMEM(shape, jnp.int32)
    picked, own_copy, words, last_row = pl.pallas_call(
        functools.partial(prepare_kernel, n_dom, q),
        out_shape=(VMEM(((n_dom - 1) * q, own_flat.shape[1]), bf16), VMEM(own_flat.shape, bf16),
                   integers(n_words, 128), VMEM((slot_count, dofs, width), bf16)),
        in_specs=[spec(pl.ANY)] * 7,
        out_specs=(spec(VMEM),) * 4,
        scratch_shapes=[integers(rows, slot_count), integers(rows, slot_count), integers(1, rows), integers(1, rows),
                        integers(1, n_dom, q), pltpu.SemaphoreType.DMA((7,))],
        compiler_params=limit,
    )(*map(in_hbm, (own_flat, columns, coarse_slots, counts, aggregate[None], requests, stiffness)))
    g_own, g_other = [], []
    for s in range(1, n_dom):
        part = picked[(s - 1) * q : s * q]
        g_own.append(lax.ppermute(part, "dom", shift_pairs(n_dom, s)))
        pairs = [(d * n_field + f, ((d + s) % n_dom) * n_field + 1 - f) for d in range(n_dom) for f in range(n_field)]
        g_other.append(lax.ppermute(part, ("dom", "field"), pairs))
    g_own = jnp.concatenate(g_own, axis=0)
    g_other = jnp.concatenate(g_other, axis=0)
    as_blocks = lambda x: in_vmem(x.reshape(x.shape[0], dofs, coarse))
    own, other = as_blocks(own_copy), as_blocks(other_flat)
    g_own, g_other = in_vmem(g_own), in_vmem(g_other)
    block = lambda *lead: (*lead, coarse, 2 * coarse)
    words, restricted, restricted_early = pl.pallas_call(
        early_kernel,
        out_shape=(SMEM(words.shape, jnp.int32), VMEM((slot_count, coarse, width), bf16),
                   VMEM((EARLY * slot_count, coarse, width), bf16)),
        in_specs=[spec(VMEM)] * 3 + [spec(pl.ANY)],
        out_specs=(spec(SMEM), spec(VMEM), spec(VMEM)),
        scratch_shapes=[VMEM((EARLY, slot_count, dofs, width), bf16), pltpu.SemaphoreType.DMA(()),
                        pltpu.SemaphoreType.DMA((EARLY,))],
        compiler_params=limit,
        cost_estimate=pl.CostEstimate(flops=10**7, bytes_accessed=10**6, transcendentals=0),
    )(in_vmem(words), in_vmem(last_row), own, in_hbm(stiffness))
    words = pltpu.with_memory_space_constraint(words, SMEM)
    restricted, restricted_early = in_vmem(restricted), in_vmem(restricted_early)
    acc = VMEM(block(2 * HALF), f32)
    table, own_part = pl.pallas_call(
        functools.partial(own_spill_kernel, n_dom, q),
        out_shape=(VMEM((n_ext, width, 2 * coarse), bf16), VMEM(block(HALF), bf16)),
        in_specs=[spec(SMEM)] + [spec(VMEM)] * 3,
        out_specs=(spec(VMEM), spec(VMEM)),
        scratch_shapes=[acc, VMEM((g_own.shape[0] * dofs // 2, 128), f32), VMEM((dofs, 128), f32)],
        compiler_params=limit,
        cost_estimate=pl.CostEstimate(flops=10**7, bytes_accessed=10**6, transcendentals=0),
    )(words, restricted, own, g_own)
    to_next = shift_pairs(lax.axis_size("blk"), 1)
    own_part = lax.ppermute(own_part, "blk", to_next)
    table, other_part = pl.pallas_call(
        functools.partial(other_spill_kernel, n_dom, q),
        out_shape=(VMEM((n_ext, width, 2 * coarse), bf16), VMEM(block(HALF), bf16)),
        in_specs=[spec(SMEM)] + [spec(VMEM)] * 4,
        out_specs=(spec(VMEM), spec(VMEM)),
        scratch_shapes=[acc, VMEM((g_own.shape[0] * dofs // 2, 128), f32), VMEM((dofs, 128), f32)],
        input_output_aliases={4: 0},
        compiler_params=limit,
        cost_estimate=pl.CostEstimate(flops=10**7, bytes_accessed=10**6, transcendentals=0),
    )(words, restricted, other, g_other, in_vmem(table))
    other_part = lax.ppermute(other_part, "blk", to_next)
    out_shape = jax.ShapeDtypeStruct(block(NC_DEV, CSLOT), bf16)
    lead = -(-EARLY * slot_count // UNROLL) * UNROLL
    later_rows, partial = pl.pallas_call(
        functools.partial(main_kernel, lead),
        out_shape=(VMEM(block(NC_DEV - 1, CSLOT), bf16), VMEM(block(CSLOT), f32)),
        in_specs=[spec(SMEM), spec(pl.ANY)] + [spec(VMEM)] * 3,
        out_specs=(spec(VMEM),) * 2,
        scratch_shapes=[SMEM((lead + rows * AVGNZ + UNROLL + slot_count,), jnp.int32),
                        VMEM(((rows - 1 - EARLY) * slot_count, dofs, width), bf16), VMEM((rows, coarse, dofs), bf16),
                        VMEM(block(NC_DEV * CSLOT + 1), f32), pltpu.SemaphoreType.DMA((rows,))],
        compiler_params=limit,
        cost_estimate=pl.CostEstimate(flops=10**9, bytes_accessed=10**7, transcendentals=0),
    )(words, in_hbm(stiffness), own, restricted_early, in_vmem(table))
    return pl.pallas_call(
        final_kernel,
        out_shape=out_shape,
        in_specs=[spec(VMEM)] * 4,
        out_specs=spec(pl.ANY),
        scratch_shapes=[VMEM(block(CSLOT), bf16), pltpu.SemaphoreType.DMA((NC_DEV + 1,))],
        compiler_params=limit,
    )(in_vmem(partial), in_vmem(own_part), in_vmem(other_part), in_vmem(later_rows))


def solution(mesh):
    in_specs = (
        P(("dom", "blk"), None, "field", None),
        P(("dom", "blk"), "field", None),
        P(("dom", "blk"), None),
        P(("dom", "blk"), None),
        P(("dom", "blk")),
        P(("dom", "blk"), None),
        P(("dom", "blk"), None, None),
    )
    out_specs = P(("dom", "blk"), None, "field", None)
    return jax.shard_map(shards, mesh=mesh, in_specs=in_specs, out_specs=out_specs, check_vma=False)
```

time: 23.1 us -> 20.1 us (0.87); the launches traced: 22.9 us -> 20.2 us
  waiting for transfers between devices: 2.16 us -> 0.01 us
  Pallas kernels: 13 us -> 11.9 us
  starting transfers between devices: 7.04 us -> 7.66 us
    ppermute x1, waiting for transfers between devices: 2.09 us -> 0.01 us  [shards(): g_other.append(lax.ppermute(part, ('dom', 'field'), pairs))]
    ppermute x1, starting transfers between devices: 1.27 us -> 0.05 us  [shards(): g_other.append(lax.ppermute(part, ('dom', 'field'), pairs))]
    ppermute x1, starting transfers between devices: 0.11 us -> 1.31 us  [shards(): g_own.append(lax.ppermute(part, 'dom', shift_pairs(n_dom, s)))]
    pallas_call x3 -> x5, Pallas kernels: 11.9 us -> 10.7 us  [the longest x1 6.51 us: shards(): pl.pallas_call(functools.partial(main_kernel, lead), out_shape=(VMEM(bloc...]
    ppermute x1 -> x2, starting transfers between devices: 3.62 us -> 4.27 us  [the longest x1 2.92 us: shards(): own_part = lax.ppermute(own_part, 'blk', to_next)]
    reshape x4 -> x2, local copies, waits for them, and re-layouts: 0.67 us -> 0.48 us  [shards(): as_blocks = lambda x: in_vmem(x.reshape(x.shape[0], dofs, coarse))]
  transfers between devices with their start and end apart: 4 -> 5, of which waited for: 2 -> 0; matrix products, arithmetic and copies ran while one was open for 2% -> 2% of each run, Pallas kernels for 43% -> 53%
where the time goes in v4:
time: 20.1 us; the launch traced here: 20.2 us
  Pallas kernels  11.9 us (59%)
  starting transfers between devices  7.66 us (38%)
  local copies, waits for them, and re-layouts  0.48 us (2%)
    pallas_call x1, Pallas kernels, shards(): pl.pallas_call(functools.partial(main_kernel, lead), out_shape=(VMEM(bloc...  6.51 us
    ppermute x1, starting transfers between devices, shards(): own_part = lax.ppermute(own_part, 'blk', to_next)  2.92 us
    ppermute x1, starting transfers between devices, shards(): other_flat = lax.ppermute(own_flat, 'field', [(0, 1), (1, 0)])  2.04 us
    pallas_call x1, Pallas kernels, shards(): pl.pallas_call(early_kernel, out_shape=(SMEM(words.shape, jnp.int32), VME...  1.57 us
    ppermute x1, starting transfers between devices, shards(): other_part = lax.ppermute(other_part, 'blk', to_next)  1.35 us
    ppermute x1, starting transfers between devices, shards(): g_own.append(lax.ppermute(part, 'dom', shift_pairs(n_dom, s)))  1.31 us
    pallas_call x1, Pallas kernels, shards(): pl.pallas_call(final_kernel, out_shape=out_shape, in_specs=[spec(VMEM)] *...  1.25 us
    pallas_call x1, Pallas kernels, shards(): pl.pallas_call(functools.partial(prepare_kernel, n_dom, q), out_shape=(VM...  1.25 us
  transfers between devices with their start and end apart: 5, of which 0 were waited for; matrix products, arithmetic and copies ran while one was open for 2% of the time, Pallas kernels for 53%

profile of v4, /device:TPU:1, one launch (start us, length us, event | category | flops | bytes accessed | tf_op | source)
XLA Modules:
  0.0 20.2 jit_solution(15316124328969466604)
XLA Ops:
  0.0 2.0 %collective-permute-start = (bf16[16,4096]{1,0:T(8,128)(2,1)}, bf16[16,4096]{1,0:T(8,128)(2,1)S(1)}, u32[]{:S(2)}, u32[]{:S(2)}) collective-permute-start(bf16[16,4096]{1,0:T(8,128)(2,1)} %bitcast.2), channel_id=1, source_target_pairs={{0,1},{1,0},{2,3},{3,2},{4,5},{5,4},{6,7},{7,6},{8,9},{9,8},{10,11... | collective-permute-start | bytes 393224 | tf_op jit(solution)/shard_map/ppermute | solution.py:267
  2.0 1.2 %shard_map.73 = (bf16[2,4096]{1,0:T(2,128)(2,1)S(1)}, bf16[16,4096]{1,0:T(8,128)(2,1)S(1)}, s32[24,128]{1,0:T(8,128)S(1)}, bf16[27,64,128]{2,1,0:T(8,128)(2,1)S(1)}) custom-call(bf16[16,4096]{1,0:T(8,128)(2,1)} %bitcast.3, s32[16,27]{1,0:T(8,128)} %columns.1, s32[16,27]{1,0:T(8,128)} %slots.1, s32[1,16]{1,0:T(1,128)} %counts.1, s32[1,16]{1,0:T(1,128)} %bitcast.4, ...), custom_call_target="tpu_custom_call" | custom-call | tf_op jit(solution)/shard_map/pallas_call | solution.py:270
  3.3 1.3 %collective-permute-start.2 = (bf16[2,4096]{1,0:T(2,128)(2,1)S(1)}, bf16[2,4096]{1,0:T(2,128)(2,1)S(1)}, u32[]{:S(2)}, u32[]{:S(2)}) collective-permute-start(bf16[2,4096]{1,0:T(2,128)(2,1)S(1)} %get-tuple-element.24), channel_id=1, source_target_pairs={{0,16},{16,0},{1,17},{17,1},{2,18},{18,2},{3,19},{19,3},{4,20},{20... | collective-permute-start | bytes 49160 | tf_op jit(solution)/shard_map/ppermute | solution.py:283
  4.6 0.0 collective-permute-start.1
  4.7 0.2 %reshape.6.own = bf16[16,64,64]{2,1,0:T(8,128)(2,1)S(1)} reshape(bf16[16,4096]{1,0:T(8,128)(2,1)S(1)} %get-tuple-element.20) | data formatting | bytes 262144 | tf_op jit(solution)/shard_map/reshape | solution.py:288
  4.9 1.6 %shard_map.74 = (s32[24,128]{1,0:T(8,128)S(4)}, bf16[27,64,128]{2,1,0:T(8,128)(2,1)S(1)}, bf16[54,64,128]{2,1,0:T(8,128)(2,1)S(1)}) custom-call(s32[24,128]{1,0:T(8,128)S(1)} %get-tuple-element.18.words_v, bf16[27,64,128]{2,1,0:T(8,128)(2,1)S(1)} %get-tuple-element.19.last_row, bf16[16,64,64]{2,1,0:T(8,128)(2,1)S(1)} %reshape.6.own, ...), custom_call_target="tpu_custom_call" | custom-call | flops 10000000 | bytes 1000000 | tf_op jit(solution)/shard_map/pallas_call | solution.py:292
  6.5 0.0 collective-permute-done.2.ghosts
  6.5 0.7 %shard_map.75 = (bf16[20,128,128]{2,1,0:T(8,128)(2,1)S(1)}, bf16[14,64,128]{2,1,0:T(8,128)(2,1)S(1)}) custom-call(s32[24,128]{1,0:T(8,128)S(4)} %get-tuple-element.21.words, bf16[27,64,128]{2,1,0:T(8,128)(2,1)S(1)} %get-tuple-element.23.restricted, bf16[16,64,64]{2,1,0:T(8,128)(2,1)S(1)} %reshape.6.own, bf16[2,4096]{1,0:T(2,128)(2,1)S(1)} %collective-permute-done.2.ghosts), custom_call_target="tpu_custom_call" | custom-call | flops 10000000 | bytes 1000000 | tf_op jit(solution)/shard_map/pallas_call | solution.py:306
  7.2 2.9 %collective-permute-start.3 = (bf16[14,64,128]{2,1,0:T(8,128)(2,1)S(1)}, bf16[14,64,128]{2,1,0:T(8,128)(2,1)S(1)}, u32[]{:S(2)}, u32[]{:S(2)}) collective-permute-start(bf16[14,64,128]{2,1,0:T(8,128)(2,1)S(1)} %get-tuple-element.28), channel_id=1, source_target_pairs={{0,2},{2,4},{4,6},{6,8},{8,10},{10,12},{12,14},{14,0},{1,3},{3,5},... | collective-permute-start | bytes 688136 | tf_op jit(solution)/shard_map/ppermute | solution.py:316
  10.1 0.0 collective-permute-done
  10.1 0.2 %reshape.7.other = bf16[16,64,64]{2,1,0:T(8,128)(2,1)S(1)} reshape(bf16[16,4096]{1,0:T(8,128)(2,1)S(1)} %collective-permute-done) | data formatting | bytes 262144 | tf_op jit(solution)/shard_map/reshape | solution.py:288
  10.4 0.0 collective-permute-done.1.ghosts
  10.4 0.7 %shard_map.76 = (bf16[20,128,128]{2,1,0:T(8,128)(2,1)S(1)}, bf16[14,64,128]{2,1,0:T(8,128)(2,1)S(1)}) custom-call(s32[24,128]{1,0:T(8,128)S(4)} %get-tuple-element.21.words, bf16[27,64,128]{2,1,0:T(8,128)(2,1)S(1)} %get-tuple-element.23.restricted, bf16[16,64,64]{2,1,0:T(8,128)(2,1)S(1)} %reshape.7.other, ...), custom_call_target="tpu_custom_call", output_to_operand_aliasing={{0}: (4, {})} | custom-call | flops 10000000 | bytes 1000000 | tf_op jit(solution)/shard_map/pallas_call | solution.py:317
  11.1 1.3 %collective-permute-start.4 = (bf16[14,64,128]{2,1,0:T(8,128)(2,1)S(1)}, bf16[14,64,128]{2,1,0:T(8,128)(2,1)S(1)}, u32[]{:S(2)}, u32[]{:S(2)}) collective-permute-start(bf16[14,64,128]{2,1,0:T(8,128)(2,1)S(1)} %get-tuple-element.29), channel_id=1, source_target_pairs={{0,2},{2,4},{4,6},{6,8},{8,10},{10,12},{12,14},{14,0},{1,3},{3,5},... | collective-permute-start | bytes 688136 | tf_op jit(solution)/shard_map/ppermute | solution.py:327
  12.4 6.5 %shard_map.77 = (bf16[3,27,64,128]{3,2,1,0:T(8,128)(2,1)S(1)}, f32[27,64,128]{2,1,0:T(8,128)S(1)}) custom-call(s32[24,128]{1,0:T(8,128)S(4)} %get-tuple-element.21.words, bf16[16,27,64,128]{3,2,1,0:T(8,128)(2,1)} %stiffness.5, bf16[16,64,64]{2,1,0:T(8,128)(2,1)S(1)} %reshape.6.own, bf16[54,64,128]{2,1,0:T(8,128)(2,1)S(1)} %get-tuple-element.22.restricted_early, ...), custom_call_target="tpu_custom_call" | custom-call | flops 1000000000 | bytes 10000000 | tf_op jit(solution)/shard_map/pallas_call | solution.py:330
  18.9 0.0 collective-permute-done.3.own_part
  18.9 0.0 collective-permute-done.4.other_part
  18.9 1.2 %shard_map.78 = bf16[4,27,64,128]{3,2,1,0:T(8,128)(2,1)} custom-call(f32[27,64,128]{2,1,0:T(8,128)S(1)} %get-tuple-element.27.partial, bf16[14,64,128]{2,1,0:T(8,128)(2,1)S(1)} %collective-permute-done.3.own_part, bf16[14,64,128]{2,1,0:T(8,128)(2,1)S(1)} %collective-permute-done.4.other_part, bf16[3,27,64,128]{3,2,1,0:T(8,128)(2,1)S(1)} %get-tuple-element.30.later_rows), custom_call_target="tpu_custom_call" | custom-call | tf_op jit(solution)/shard_map/pallas_call | solution.py:341
Async XLA Ops:
  0.0 10.1 %collective-permute-start = (bf16[16,4096]{1,0:T(8,128)(2,1)}, bf16[16,4096]{1,0:T(8,128)(2,1)S(1)}, u32[]{:S(2)}, u32[]{:S(2)}) collective-permute-start(bf16[16,4096]{1,0:T(8,128)(2,1)} %bitcast.2), channel_id=1, source_target_pairs={{0,1},{1,0},{2,3},{3,2},{4,5},{5,4},{6,7},{7,6},{8,9},{9,8},{10,11... | collective-permute-start | bytes 393224 | tf_op jit(solution)/shard_map/ppermute | solution.py:267
  3.3 3.2 %collective-permute-start.2 = (bf16[2,4096]{1,0:T(2,128)(2,1)S(1)}, bf16[2,4096]{1,0:T(2,128)(2,1)S(1)}, u32[]{:S(2)}, u32[]{:S(2)}) collective-permute-start(bf16[2,4096]{1,0:T(2,128)(2,1)S(1)} %get-tuple-element.24), channel_id=1, source_target_pairs={{0,16},{16,0},{1,17},{17,1},{2,18},{18,2},{3,19},{19,3},{4,20},{20... | collective-permute-start | bytes 49160 | tf_op jit(solution)/shard_map/ppermute | solution.py:283
  4.6 5.8 %collective-permute-start.1 = (bf16[2,4096]{1,0:T(2,128)(2,1)S(1)}, bf16[2,4096]{1,0:T(2,128)(2,1)S(1)}, u32[]{:S(2)}, u32[]{:S(2)}) collective-permute-start(bf16[2,4096]{1,0:T(2,128)(2,1)S(1)} %get-tuple-element.24), channel_id=1, source_target_pairs={{0,17},{1,16},{16,1},{17,0},{2,19},{3,18},{18,3},{19,2},{4,21},{5,... | collective-permute-start | bytes 49160 | tf_op jit(solution)/shard_map/ppermute | solution.py:285
  7.2 11.7 %collective-permute-start.3 = (bf16[14,64,128]{2,1,0:T(8,128)(2,1)S(1)}, bf16[14,64,128]{2,1,0:T(8,128)(2,1)S(1)}, u32[]{:S(2)}, u32[]{:S(2)}) collective-permute-start(bf16[14,64,128]{2,1,0:T(8,128)(2,1)S(1)} %get-tuple-element.28), channel_id=1, source_target_pairs={{0,2},{2,4},{4,6},{6,8},{8,10},{10,12},{12,14},{14,0},{1,3},{3,5},... | collective-permute-start | bytes 688136 | tf_op jit(solution)/shard_map/ppermute | solution.py:316
  11.1 7.9 %collective-permute-start.4 = (bf16[14,64,128]{2,1,0:T(8,128)(2,1)S(1)}, bf16[14,64,128]{2,1,0:T(8,128)(2,1)S(1)}, u32[]{:S(2)}, u32[]{:S(2)}) collective-permute-start(bf16[14,64,128]{2,1,0:T(8,128)(2,1)S(1)} %get-tuple-element.29), channel_id=1, source_target_pairs={{0,2},{2,4},{4,6},{6,8},{8,10},{10,12},{12,14},{14,0},{1,3},{3,5},... | collective-permute-start | bytes 688136 | tf_op jit(solution)/shard_map/ppermute | solution.py:327

commit v5 on v4

--- a/solution.py
+++ b/solution.py
@@ -11,7 +11,9 @@
 NC_DEV = 4
 HALF = 14
 AVGNZ = 16
-UNROLL = 32
+CHUNK = 64
+REST = 16
+FIRST = 32
 EARLY = 2
 COLUMN_BIT = 10
 SEG_BIT = 16
@@ -177,7 +179,7 @@
     base = 0
     for i in range(rows - 1):
         if i == EARLY:
-            for k in range(UNROLL):
+            for k in range(FIRST):
                 listed[base + k] = UNUSED << SEG_BIT
             first_length = base
             base = lead
@@ -185,7 +187,7 @@
         for k in range(slot_count):
             listed[base + k] = words[i, k] + offset
         base = base + words[rows, i]
-    for k in range(UNROLL):
+    for k in range(REST):
         listed[base + k] = (UNUSED << SEG_BIT) + (rows - 2) * slot_count
     return first_length, base - lead
 
@@ -210,15 +212,15 @@
         for w, z in zip(taken, products):
             acc[w >> SEG_BIT] += z
 
-    @pl.loop(0, (first_length + UNROLL - 1) // UNROLL)
+    @pl.loop(0, (first_length + FIRST - 1) // FIRST)
     def _(c):
-        taken = [listed[c * UNROLL + u] for u in range(UNROLL)]
+        taken = [listed[c * FIRST + u] for u in range(FIRST)]
         add(taken, [restricted_early[block_of(w)] for w in taken])
 
-    def chunk(c, arrived):
-        taken = [listed[lead + c * UNROLL + u] for u in range(UNROLL)]
+    def chunk(start, size, arrived):
+        taken = [listed[lead + start + u] for u in range(size)]
         blocks = [block_of(w) for w in taken]
-        needed = blocks[UNROLL - 1] // slot_count + 1
+        needed = blocks[size - 1] // slot_count + 1
 
         @pl.loop(arrived, needed)
         def _(i):
@@ -230,7 +232,10 @@
         ])
         return needed
 
-    lax.fori_loop(0, (second_length + UNROLL - 1) // UNROLL, chunk, EARLY)
+    whole = second_length // CHUNK
+    left = second_length - whole * CHUNK
+    arrived = lax.fori_loop(0, whole, lambda c, got: chunk(c * CHUNK, CHUNK, got), EARLY)
+    lax.fori_loop(0, (left + REST - 1) // REST, lambda c, got: chunk(whole * CHUNK + c * REST, REST, got), arrived)
     for c in range(1, NC_DEV):
         later_rows[c - 1] = acc[c * CSLOT : (c + 1) * CSLOT].astype(bf16)
     first_row[...] = acc[0:CSLOT]
@@ -326,13 +331,13 @@
     )(words, restricted, other, g_other, in_vmem(table))
     other_part = lax.ppermute(other_part, "blk", to_next)
     out_shape = jax.ShapeDtypeStruct(block(NC_DEV, CSLOT), bf16)
-    lead = -(-EARLY * slot_count // UNROLL) * UNROLL
+    lead = EARLY * slot_count + FIRST
     later_rows, partial = pl.pallas_call(
         functools.partial(main_kernel, lead),
         out_shape=(VMEM(block(NC_DEV - 1, CSLOT), bf16), VMEM(block(CSLOT), f32)),
         in_specs=[spec(SMEM), spec(pl.ANY)] + [spec(VMEM)] * 3,
         out_specs=(spec(VMEM),) * 2,
-        scratch_shapes=[SMEM((lead + rows * AVGNZ + UNROLL + slot_count,), jnp.int32),
+        scratch_shapes=[SMEM((lead + rows * AVGNZ + REST + slot_count,), jnp.int32),
                         VMEM(((rows - 1 - EARLY) * slot_count, dofs, width), bf16), VMEM((rows, coarse, dofs), bf16),
                         VMEM(block(NC_DEV * CSLOT + 1), f32), pltpu.SemaphoreType.DMA((rows,))],
         compiler_params=limit,

time: 20.1 us -> 20.5 us (1.020); the launches traced: 20.2 us -> 20.3 us
  no operation moved by 1% of the time
where the time goes in v5:
time: 20.5 us; the launch traced here: 20.3 us
  Pallas kernels  12.1 us (59%)
  starting transfers between devices  7.63 us (37%)
  local copies, waits for them, and re-layouts  0.48 us (2%)
    pallas_call x1, Pallas kernels, shards(): pl.pallas_call(functools.partial(main_kernel, lead), out_shape=(VMEM(bloc...  6.62 us
    ppermute x1, starting transfers between devices, shards(): own_part = lax.ppermute(own_part, 'blk', to_next)  2.9 us
    ppermute x1, starting transfers between devices, shards(): other_flat = lax.ppermute(own_flat, 'field', [(0, 1), (1, 0)])  2.04 us
    pallas_call x1, Pallas kernels, shards(): pl.pallas_call(early_kernel, out_shape=(SMEM(words.shape, jnp.int32), VME...  1.57 us
    ppermute x1, starting transfers between devices, shards(): other_part = lax.ppermute(other_part, 'blk', to_next)  1.34 us
    ppermute x1, starting transfers between devices, shards(): g_own.append(lax.ppermute(part, 'dom', shift_pairs(n_dom, s)))  1.31 us
    pallas_call x1, Pallas kernels, shards(): pl.pallas_call(final_kernel, out_shape=out_shape, in_specs=[spec(VMEM)] *...  1.25 us
    pallas_call x1, Pallas kernels, shards(): pl.pallas_call(functools.partial(prepare_kernel, n_dom, q), out_shape=(VM...  1.25 us
  transfers between devices with their start and end apart: 5, of which 0 were waited for; matrix products, arithmetic and copies ran while one was open for 2% of the time, Pallas kernels for 53%

profile of v5, /device:TPU:1, one launch (start us, length us, event | category | flops | bytes accessed | tf_op | source)
XLA Modules:
  0.0 20.3 jit_solution(15514836004780320224)
XLA Ops:
  0.0 2.0 %collective-permute-start = (bf16[16,4096]{1,0:T(8,128)(2,1)}, bf16[16,4096]{1,0:T(8,128)(2,1)S(1)}, u32[]{:S(2)}, u32[]{:S(2)}) collective-permute-start(bf16[16,4096]{1,0:T(8,128)(2,1)} %bitcast.2), channel_id=1, source_target_pairs={{0,1},{1,0},{2,3},{3,2},{4,5},{5,4},{6,7},{7,6},{8,9},{9,8},{10,11... | collective-permute-start | bytes 393224 | tf_op jit(solution)/shard_map/ppermute | solution.py:272
  2.0 1.2 %shard_map.73 = (bf16[2,4096]{1,0:T(2,128)(2,1)S(1)}, bf16[16,4096]{1,0:T(8,128)(2,1)S(1)}, s32[24,128]{1,0:T(8,128)S(1)}, bf16[27,64,128]{2,1,0:T(8,128)(2,1)S(1)}) custom-call(bf16[16,4096]{1,0:T(8,128)(2,1)} %bitcast.3, s32[16,27]{1,0:T(8,128)} %columns.1, s32[16,27]{1,0:T(8,128)} %slots.1, s32[1,16]{1,0:T(1,128)} %counts.1, s32[1,16]{1,0:T(1,128)} %bitcast.4, ...), custom_call_target="tpu_custom_call" | custom-call | tf_op jit(solution)/shard_map/pallas_call | solution.py:275
  3.3 1.3 %collective-permute-start.2 = (bf16[2,4096]{1,0:T(2,128)(2,1)S(1)}, bf16[2,4096]{1,0:T(2,128)(2,1)S(1)}, u32[]{:S(2)}, u32[]{:S(2)}) collective-permute-start(bf16[2,4096]{1,0:T(2,128)(2,1)S(1)} %get-tuple-element.24), channel_id=1, source_target_pairs={{0,16},{16,0},{1,17},{17,1},{2,18},{18,2},{3,19},{19,3},{4,20},{20... | collective-permute-start | bytes 49160 | tf_op jit(solution)/shard_map/ppermute | solution.py:288
  4.6 0.0 collective-permute-start.1
  4.7 0.2 %reshape.6.own = bf16[16,64,64]{2,1,0:T(8,128)(2,1)S(1)} reshape(bf16[16,4096]{1,0:T(8,128)(2,1)S(1)} %get-tuple-element.20) | data formatting | bytes 262144 | tf_op jit(solution)/shard_map/reshape | solution.py:293
  4.9 1.6 %shard_map.74 = (s32[24,128]{1,0:T(8,128)S(4)}, bf16[27,64,128]{2,1,0:T(8,128)(2,1)S(1)}, bf16[54,64,128]{2,1,0:T(8,128)(2,1)S(1)}) custom-call(s32[24,128]{1,0:T(8,128)S(1)} %get-tuple-element.18.words_v, bf16[27,64,128]{2,1,0:T(8,128)(2,1)S(1)} %get-tuple-element.19.last_row, bf16[16,64,64]{2,1,0:T(8,128)(2,1)S(1)} %reshape.6.own, ...), custom_call_target="tpu_custom_call" | custom-call | flops 10000000 | bytes 1000000 | tf_op jit(solution)/shard_map/pallas_call | solution.py:297
  6.5 0.0 collective-permute-done.2.ghosts
  6.5 0.7 %shard_map.75 = (bf16[20,128,128]{2,1,0:T(8,128)(2,1)S(1)}, bf16[14,64,128]{2,1,0:T(8,128)(2,1)S(1)}) custom-call(s32[24,128]{1,0:T(8,128)S(4)} %get-tuple-element.21.words, bf16[27,64,128]{2,1,0:T(8,128)(2,1)S(1)} %get-tuple-element.23.restricted, bf16[16,64,64]{2,1,0:T(8,128)(2,1)S(1)} %reshape.6.own, bf16[2,4096]{1,0:T(2,128)(2,1)S(1)} %collective-permute-done.2.ghosts), custom_call_target="tpu_custom_call" | custom-call | flops 10000000 | bytes 1000000 | tf_op jit(solution)/shard_map/pallas_call | solution.py:311
  7.2 2.9 %collective-permute-start.3 = (bf16[14,64,128]{2,1,0:T(8,128)(2,1)S(1)}, bf16[14,64,128]{2,1,0:T(8,128)(2,1)S(1)}, u32[]{:S(2)}, u32[]{:S(2)}) collective-permute-start(bf16[14,64,128]{2,1,0:T(8,128)(2,1)S(1)} %get-tuple-element.28), channel_id=1, source_target_pairs={{0,2},{2,4},{4,6},{6,8},{8,10},{10,12},{12,14},{14,0},{1,3},{3,5},... | collective-permute-start | bytes 688136 | tf_op jit(solution)/shard_map/ppermute | solution.py:321
  10.1 0.0 collective-permute-done
  10.1 0.2 %reshape.7.other = bf16[16,64,64]{2,1,0:T(8,128)(2,1)S(1)} reshape(bf16[16,4096]{1,0:T(8,128)(2,1)S(1)} %collective-permute-done) | data formatting | bytes 262144 | tf_op jit(solution)/shard_map/reshape | solution.py:293
  10.4 0.0 collective-permute-done.1.ghosts
  10.4 0.7 %shard_map.76 = (bf16[20,128,128]{2,1,0:T(8,128)(2,1)S(1)}, bf16[14,64,128]{2,1,0:T(8,128)(2,1)S(1)}) custom-call(s32[24,128]{1,0:T(8,128)S(4)} %get-tuple-element.21.words, bf16[27,64,128]{2,1,0:T(8,128)(2,1)S(1)} %get-tuple-element.23.restricted, bf16[16,64,64]{2,1,0:T(8,128)(2,1)S(1)} %reshape.7.other, ...), custom_call_target="tpu_custom_call", output_to_operand_aliasing={{0}: (4, {})} | custom-call | flops 10000000 | bytes 1000000 | tf_op jit(solution)/shard_map/pallas_call | solution.py:322
  11.1 1.3 %collective-permute-start.4 = (bf16[14,64,128]{2,1,0:T(8,128)(2,1)S(1)}, bf16[14,64,128]{2,1,0:T(8,128)(2,1)S(1)}, u32[]{:S(2)}, u32[]{:S(2)}) collective-permute-start(bf16[14,64,128]{2,1,0:T(8,128)(2,1)S(1)} %get-tuple-element.29), channel_id=1, source_target_pairs={{0,2},{2,4},{4,6},{6,8},{8,10},{10,12},{12,14},{14,0},{1,3},{3,5},... | collective-permute-start | bytes 688136 | tf_op jit(solution)/shard_map/ppermute | solution.py:332
  12.4 6.6 %shard_map.77 = (bf16[3,27,64,128]{3,2,1,0:T(8,128)(2,1)S(1)}, f32[27,64,128]{2,1,0:T(8,128)S(1)}) custom-call(s32[24,128]{1,0:T(8,128)S(4)} %get-tuple-element.21.words, bf16[16,27,64,128]{3,2,1,0:T(8,128)(2,1)} %stiffness.5, bf16[16,64,64]{2,1,0:T(8,128)(2,1)S(1)} %reshape.6.own, bf16[54,64,128]{2,1,0:T(8,128)(2,1)S(1)} %get-tuple-element.22.restricted_early, ...), custom_call_target="tpu_custom_call" | custom-call | flops 1000000000 | bytes 10000000 | tf_op jit(solution)/shard_map/pallas_call | solution.py:335
  19.0 0.0 collective-permute-done.3.own_part
  19.0 0.0 collective-permute-done.4.other_part
  19.0 1.2 %shard_map.78 = bf16[4,27,64,128]{3,2,1,0:T(8,128)(2,1)} custom-call(f32[27,64,128]{2,1,0:T(8,128)S(1)} %get-tuple-element.27.partial, bf16[14,64,128]{2,1,0:T(8,128)(2,1)S(1)} %collective-permute-done.3.own_part, bf16[14,64,128]{2,1,0:T(8,128)(2,1)S(1)} %collective-permute-done.4.other_part, bf16[3,27,64,128]{3,2,1,0:T(8,128)(2,1)S(1)} %get-tuple-element.30.later_rows), custom_call_target="tpu_custom_call" | custom-call | tf_op jit(solution)/shard_map/pallas_call | solution.py:346
Async XLA Ops:
  0.0 10.1 %collective-permute-start = (bf16[16,4096]{1,0:T(8,128)(2,1)}, bf16[16,4096]{1,0:T(8,128)(2,1)S(1)}, u32[]{:S(2)}, u32[]{:S(2)}) collective-permute-start(bf16[16,4096]{1,0:T(8,128)(2,1)} %bitcast.2), channel_id=1, source_target_pairs={{0,1},{1,0},{2,3},{3,2},{4,5},{5,4},{6,7},{7,6},{8,9},{9,8},{10,11... | collective-permute-start | bytes 393224 | tf_op jit(solution)/shard_map/ppermute | solution.py:272
  3.3 3.2 %collective-permute-start.2 = (bf16[2,4096]{1,0:T(2,128)(2,1)S(1)}, bf16[2,4096]{1,0:T(2,128)(2,1)S(1)}, u32[]{:S(2)}, u32[]{:S(2)}) collective-permute-start(bf16[2,4096]{1,0:T(2,128)(2,1)S(1)} %get-tuple-element.24), channel_id=1, source_target_pairs={{0,16},{16,0},{1,17},{17,1},{2,18},{18,2},{3,19},{19,3},{4,20},{20... | collective-permute-start | bytes 49160 | tf_op jit(solution)/shard_map/ppermute | solution.py:288
  4.6 5.8 %collective-permute-start.1 = (bf16[2,4096]{1,0:T(2,128)(2,1)S(1)}, bf16[2,4096]{1,0:T(2,128)(2,1)S(1)}, u32[]{:S(2)}, u32[]{:S(2)}) collective-permute-start(bf16[2,4096]{1,0:T(2,128)(2,1)S(1)} %get-tuple-element.24), channel_id=1, source_target_pairs={{0,17},{1,16},{16,1},{17,0},{2,19},{3,18},{18,3},{19,2},{4,21},{5,... | collective-permute-start | bytes 49160 | tf_op jit(solution)/shard_map/ppermute | solution.py:290
  7.2 11.8 %collective-permute-start.3 = (bf16[14,64,128]{2,1,0:T(8,128)(2,1)S(1)}, bf16[14,64,128]{2,1,0:T(8,128)(2,1)S(1)}, u32[]{:S(2)}, u32[]{:S(2)}) collective-permute-start(bf16[14,64,128]{2,1,0:T(8,128)(2,1)S(1)} %get-tuple-element.28), channel_id=1, source_target_pairs={{0,2},{2,4},{4,6},{6,8},{8,10},{10,12},{12,14},{14,0},{1,3},{3,5},... | collective-permute-start | bytes 688136 | tf_op jit(solution)/shard_map/ppermute | solution.py:321
  11.1 8.0 %collective-permute-start.4 = (bf16[14,64,128]{2,1,0:T(8,128)(2,1)S(1)}, bf16[14,64,128]{2,1,0:T(8,128)(2,1)S(1)}, u32[]{:S(2)}, u32[]{:S(2)}) collective-permute-start(bf16[14,64,128]{2,1,0:T(8,128)(2,1)S(1)} %get-tuple-element.29), channel_id=1, source_target_pairs={{0,2},{2,4},{4,6},{6,8},{8,10},{10,12},{12,14},{14,0},{1,3},{3,5},... | collective-permute-start | bytes 688136 | tf_op jit(solution)/shard_map/ppermute | solution.py:332

commit v6 on v5

--- a/solution.py
+++ b/solution.py
@@ -11,7 +11,8 @@
 NC_DEV = 4
 HALF = 14
 AVGNZ = 16
-CHUNK = 64
+CHUNK = 96
+GROUP = 16
 REST = 16
 FIRST = 32
 EARLY = 2
@@ -109,7 +110,7 @@
         pairs = tiles[pl.ds(r, dofs // 2, stride=count)]
         lines[pl.ds(0, dofs // 2, stride=2)] = pairs
         lines[pl.ds(1, dofs // 2, stride=2)] = pltpu.roll(pairs, 64, 1)
-        blocks.append(lines[:, 0:64].astype(bf16))
+        blocks.append(lines[0:dofs, 0:64].astype(bf16))
     return blocks
 
 
@@ -226,16 +227,22 @@
         def _(i):
             row_copy(i).wait()
 
-        add(taken, [
-            jnp.dot(restrict[b // slot_count], stiff[b - EARLY * slot_count], preferred_element_type=f32).astype(bf16)
-            for b in blocks
-        ])
+        held = None
+        for g in range(0, size, GROUP):
+            restricted = [
+                jnp.dot(restrict[b // slot_count], stiff[b - EARLY * slot_count], preferred_element_type=f32).astype(bf16)
+                for b in blocks[g : g + GROUP]
+            ]
+            if held is not None:
+                add(*held)
+            held = taken[g : g + GROUP], restricted
+        add(*held)
         return needed
 
     whole = second_length // CHUNK
-    left = second_length - whole * CHUNK
-    arrived = lax.fori_loop(0, whole, lambda c, got: chunk(c * CHUNK, CHUNK, got), EARLY)
-    lax.fori_loop(0, (left + REST - 1) // REST, lambda c, got: chunk(whole * CHUNK + c * REST, REST, got), arrived)
+    small = (second_length - whole * CHUNK + REST - 1) // REST
+    arrived = lax.fori_loop(0, small, lambda c, got: chunk(c * REST, REST, got), EARLY)
+    lax.fori_loop(0, whole, lambda c, got: chunk(small * REST + c * CHUNK, CHUNK, got), arrived)
     for c in range(1, NC_DEV):
         later_rows[c - 1] = acc[c * CSLOT : (c + 1) * CSLOT].astype(bf16)
     first_row[...] = acc[0:CSLOT]
@@ -308,12 +315,13 @@
     words = pltpu.with_memory_space_constraint(words, SMEM)
     restricted, restricted_early = in_vmem(restricted), in_vmem(restricted_early)
     acc = VMEM(block(2 * HALF), f32)
+    unfolding = VMEM((g_own.shape[0] * (dofs // 2 + 4), 128), f32), VMEM((dofs + 8, 128), f32)
     table, own_part = pl.pallas_call(
         functools.partial(own_spill_kernel, n_dom, q),
         out_shape=(VMEM((n_ext, width, 2 * coarse), bf16), VMEM(block(HALF), bf16)),
         in_specs=[spec(SMEM)] + [spec(VMEM)] * 3,
         out_specs=(spec(VMEM), spec(VMEM)),
-        scratch_shapes=[acc, VMEM((g_own.shape[0] * dofs // 2, 128), f32), VMEM((dofs, 128), f32)],
+        scratch_shapes=[acc, *unfolding],
         compiler_params=limit,
         cost_estimate=pl.CostEstimate(flops=10**7, bytes_accessed=10**6, transcendentals=0),
     )(words, restricted, own, g_own)
@@ -324,7 +332,7 @@
         out_shape=(VMEM((n_ext, width, 2 * coarse), bf16), VMEM(block(HALF), bf16)),
         in_specs=[spec(SMEM)] + [spec(VMEM)] * 4,
         out_specs=(spec(VMEM), spec(VMEM)),
-        scratch_shapes=[acc, VMEM((g_own.shape[0] * dofs // 2, 128), f32), VMEM((dofs, 128), f32)],
+        scratch_shapes=[acc, *unfolding],
         input_output_aliases={4: 0},
         compiler_params=limit,
         cost_estimate=pl.CostEstimate(flops=10**7, bytes_accessed=10**6, transcendentals=0),

time: 20.5 us -> 19.9 us (0.971)
  Pallas kernels: 12.1 us -> 11.3 us
    pallas_call x1, Pallas kernels: 6.62 us -> 5.9 us  [shards(): pl.pallas_call(functools.partial(main_kernel, lead), out_shape=(VMEM(bloc...]
  transfers between devices with their start and end apart: 5 -> 5, of which waited for: 0 -> 0; matrix products, arithmetic and copies ran while one was open for 2% -> 2% of each run, Pallas kernels for 53% -> 51%
where the time goes in v6:
time: 19.9 us; the launch traced here: 19.6 us
  Pallas kernels  11.3 us (57%)
  starting transfers between devices  7.65 us (38%)
  local copies, waits for them, and re-layouts  0.48 us (2%)
    pallas_call x1, Pallas kernels, shards(): pl.pallas_call(functools.partial(main_kernel, lead), out_shape=(VMEM(bloc...  5.9 us
    ppermute x1, starting transfers between devices, shards(): own_part = lax.ppermute(own_part, 'blk', to_next)  2.91 us
    ppermute x1, starting transfers between devices, shards(): other_flat = lax.ppermute(own_flat, 'field', [(0, 1), (1, 0)])  2.04 us
    pallas_call x1, Pallas kernels, shards(): pl.pallas_call(early_kernel, out_shape=(SMEM(words.shape, jnp.int32), VME...  1.57 us
    ppermute x1, starting transfers between devices, shards(): other_part = lax.ppermute(other_part, 'blk', to_next)  1.35 us
    ppermute x1, starting transfers between devices, shards(): g_own.append(lax.ppermute(part, 'dom', shift_pairs(n_dom, s)))  1.31 us
    pallas_call x1, Pallas kernels, shards(): pl.pallas_call(final_kernel, out_shape=out_shape, in_specs=[spec(VMEM)] *...  1.25 us
    pallas_call x1, Pallas kernels, shards(): pl.pallas_call(functools.partial(prepare_kernel, n_dom, q), out_shape=(VM...  1.25 us
  transfers between devices with their start and end apart: 5, of which 0 were waited for; matrix products, arithmetic and copies ran while one was open for 2% of the time, Pallas kernels for 51%

profile of v6, /device:TPU:1, one launch (start us, length us, event | category | flops | bytes accessed | tf_op | source)
XLA Modules:
  0.0 19.6 jit_solution(7154133205145432508)
XLA Ops:
  0.0 2.0 %collective-permute-start = (bf16[16,4096]{1,0:T(8,128)(2,1)}, bf16[16,4096]{1,0:T(8,128)(2,1)S(1)}, u32[]{:S(2)}, u32[]{:S(2)}) collective-permute-start(bf16[16,4096]{1,0:T(8,128)(2,1)} %bitcast.2), channel_id=1, source_target_pairs={{0,1},{1,0},{2,3},{3,2},{4,5},{5,4},{6,7},{7,6},{8,9},{9,8},{10,11... | collective-permute-start | bytes 393224 | tf_op jit(solution)/shard_map/ppermute | solution.py:279
  2.0 1.2 %shard_map.73 = (bf16[2,4096]{1,0:T(2,128)(2,1)S(1)}, bf16[16,4096]{1,0:T(8,128)(2,1)S(1)}, s32[24,128]{1,0:T(8,128)S(1)}, bf16[27,64,128]{2,1,0:T(8,128)(2,1)S(1)}) custom-call(bf16[16,4096]{1,0:T(8,128)(2,1)} %bitcast.3, s32[16,27]{1,0:T(8,128)} %columns.1, s32[16,27]{1,0:T(8,128)} %slots.1, s32[1,16]{1,0:T(1,128)} %counts.1, s32[1,16]{1,0:T(1,128)} %bitcast.4, ...), custom_call_target="tpu_custom_call" | custom-call | tf_op jit(solution)/shard_map/pallas_call | solution.py:282
  3.3 1.3 %collective-permute-start.2 = (bf16[2,4096]{1,0:T(2,128)(2,1)S(1)}, bf16[2,4096]{1,0:T(2,128)(2,1)S(1)}, u32[]{:S(2)}, u32[]{:S(2)}) collective-permute-start(bf16[2,4096]{1,0:T(2,128)(2,1)S(1)} %get-tuple-element.24), channel_id=1, source_target_pairs={{0,16},{16,0},{1,17},{17,1},{2,18},{18,2},{3,19},{19,3},{4,20},{20... | collective-permute-start | bytes 49160 | tf_op jit(solution)/shard_map/ppermute | solution.py:295
  4.6 0.0 collective-permute-start.1
  4.7 0.2 %reshape.6.own = bf16[16,64,64]{2,1,0:T(8,128)(2,1)S(1)} reshape(bf16[16,4096]{1,0:T(8,128)(2,1)S(1)} %get-tuple-element.20) | data formatting | bytes 262144 | tf_op jit(solution)/shard_map/reshape | solution.py:300
  4.9 1.6 %shard_map.74 = (s32[24,128]{1,0:T(8,128)S(4)}, bf16[27,64,128]{2,1,0:T(8,128)(2,1)S(1)}, bf16[54,64,128]{2,1,0:T(8,128)(2,1)S(1)}) custom-call(s32[24,128]{1,0:T(8,128)S(1)} %get-tuple-element.18.words_v, bf16[27,64,128]{2,1,0:T(8,128)(2,1)S(1)} %get-tuple-element.19.last_row, bf16[16,64,64]{2,1,0:T(8,128)(2,1)S(1)} %reshape.6.own, ...), custom_call_target="tpu_custom_call" | custom-call | flops 10000000 | bytes 1000000 | tf_op jit(solution)/shard_map/pallas_call | solution.py:304
  6.5 0.0 collective-permute-done.2.ghosts
  6.5 0.7 %shard_map.75 = (bf16[20,128,128]{2,1,0:T(8,128)(2,1)S(1)}, bf16[14,64,128]{2,1,0:T(8,128)(2,1)S(1)}) custom-call(s32[24,128]{1,0:T(8,128)S(4)} %get-tuple-element.21.words, bf16[27,64,128]{2,1,0:T(8,128)(2,1)S(1)} %get-tuple-element.23.restricted, bf16[16,64,64]{2,1,0:T(8,128)(2,1)S(1)} %reshape.6.own, bf16[2,4096]{1,0:T(2,128)(2,1)S(1)} %collective-permute-done.2.ghosts), custom_call_target="tpu_custom_call" | custom-call | flops 10000000 | bytes 1000000 | tf_op jit(solution)/shard_map/pallas_call | solution.py:319
  7.2 2.9 %collective-permute-start.3 = (bf16[14,64,128]{2,1,0:T(8,128)(2,1)S(1)}, bf16[14,64,128]{2,1,0:T(8,128)(2,1)S(1)}, u32[]{:S(2)}, u32[]{:S(2)}) collective-permute-start(bf16[14,64,128]{2,1,0:T(8,128)(2,1)S(1)} %get-tuple-element.28), channel_id=1, source_target_pairs={{0,2},{2,4},{4,6},{6,8},{8,10},{10,12},{12,14},{14,0},{1,3},{3,5},... | collective-permute-start | bytes 688136 | tf_op jit(solution)/shard_map/ppermute | solution.py:329
  10.1 0.0 collective-permute-done
  10.1 0.2 %reshape.7.other = bf16[16,64,64]{2,1,0:T(8,128)(2,1)S(1)} reshape(bf16[16,4096]{1,0:T(8,128)(2,1)S(1)} %collective-permute-done) | data formatting | bytes 262144 | tf_op jit(solution)/shard_map/reshape | solution.py:300
  10.4 0.0 collective-permute-done.1.ghosts
  10.4 0.7 %shard_map.76 = (bf16[20,128,128]{2,1,0:T(8,128)(2,1)S(1)}, bf16[14,64,128]{2,1,0:T(8,128)(2,1)S(1)}) custom-call(s32[24,128]{1,0:T(8,128)S(4)} %get-tuple-element.21.words, bf16[27,64,128]{2,1,0:T(8,128)(2,1)S(1)} %get-tuple-element.23.restricted, bf16[16,64,64]{2,1,0:T(8,128)(2,1)S(1)} %reshape.7.other, ...), custom_call_target="tpu_custom_call", output_to_operand_aliasing={{0}: (4, {})} | custom-call | flops 10000000 | bytes 1000000 | tf_op jit(solution)/shard_map/pallas_call | solution.py:330
  11.0 1.3 %collective-permute-start.4 = (bf16[14,64,128]{2,1,0:T(8,128)(2,1)S(1)}, bf16[14,64,128]{2,1,0:T(8,128)(2,1)S(1)}, u32[]{:S(2)}, u32[]{:S(2)}) collective-permute-start(bf16[14,64,128]{2,1,0:T(8,128)(2,1)S(1)} %get-tuple-element.29), channel_id=1, source_target_pairs={{0,2},{2,4},{4,6},{6,8},{8,10},{10,12},{12,14},{14,0},{1,3},{3,5},... | collective-permute-start | bytes 688136 | tf_op jit(solution)/shard_map/ppermute | solution.py:340
  12.4 5.9 %shard_map.77 = (bf16[3,27,64,128]{3,2,1,0:T(8,128)(2,1)S(1)}, f32[27,64,128]{2,1,0:T(8,128)S(1)}) custom-call(s32[24,128]{1,0:T(8,128)S(4)} %get-tuple-element.21.words, bf16[16,27,64,128]{3,2,1,0:T(8,128)(2,1)} %stiffness.5, bf16[16,64,64]{2,1,0:T(8,128)(2,1)S(1)} %reshape.6.own, bf16[54,64,128]{2,1,0:T(8,128)(2,1)S(1)} %get-tuple-element.22.restricted_early, ...), custom_call_target="tpu_custom_call" | custom-call | flops 1000000000 | bytes 10000000 | tf_op jit(solution)/shard_map/pallas_call | solution.py:343
  18.3 0.0 collective-permute-done.3.own_part
  18.3 0.0 collective-permute-done.4.other_part
  18.3 1.2 %shard_map.78 = bf16[4,27,64,128]{3,2,1,0:T(8,128)(2,1)} custom-call(f32[27,64,128]{2,1,0:T(8,128)S(1)} %get-tuple-element.27.partial, bf16[14,64,128]{2,1,0:T(8,128)(2,1)S(1)} %collective-permute-done.3.own_part, bf16[14,64,128]{2,1,0:T(8,128)(2,1)S(1)} %collective-permute-done.4.other_part, bf16[3,27,64,128]{3,2,1,0:T(8,128)(2,1)S(1)} %get-tuple-element.30.later_rows), custom_call_target="tpu_custom_call" | custom-call | tf_op jit(solution)/shard_map/pallas_call | solution.py:354
Async XLA Ops:
  0.0 10.1 %collective-permute-start = (bf16[16,4096]{1,0:T(8,128)(2,1)}, bf16[16,4096]{1,0:T(8,128)(2,1)S(1)}, u32[]{:S(2)}, u32[]{:S(2)}) collective-permute-start(bf16[16,4096]{1,0:T(8,128)(2,1)} %bitcast.2), channel_id=1, source_target_pairs={{0,1},{1,0},{2,3},{3,2},{4,5},{5,4},{6,7},{7,6},{8,9},{9,8},{10,11... | collective-permute-start | bytes 393224 | tf_op jit(solution)/shard_map/ppermute | solution.py:279
  3.3 3.2 %collective-permute-start.2 = (bf16[2,4096]{1,0:T(2,128)(2,1)S(1)}, bf16[2,4096]{1,0:T(2,128)(2,1)S(1)}, u32[]{:S(2)}, u32[]{:S(2)}) collective-permute-start(bf16[2,4096]{1,0:T(2,128)(2,1)S(1)} %get-tuple-element.24), channel_id=1, source_target_pairs={{0,16},{16,0},{1,17},{17,1},{2,18},{18,2},{3,19},{19,3},{4,20},{20... | collective-permute-start | bytes 49160 | tf_op jit(solution)/shard_map/ppermute | solution.py:295
  4.6 5.8 %collective-permute-start.1 = (bf16[2,4096]{1,0:T(2,128)(2,1)S(1)}, bf16[2,4096]{1,0:T(2,128)(2,1)S(1)}, u32[]{:S(2)}, u32[]{:S(2)}) collective-permute-start(bf16[2,4096]{1,0:T(2,128)(2,1)S(1)} %get-tuple-element.24), channel_id=1, source_target_pairs={{0,17},{1,16},{16,1},{17,0},{2,19},{3,18},{18,3},{19,2},{4,21},{5,... | collective-permute-start | bytes 49160 | tf_op jit(solution)/shard_map/ppermute | solution.py:297
  7.2 11.1 %collective-permute-start.3 = (bf16[14,64,128]{2,1,0:T(8,128)(2,1)S(1)}, bf16[14,64,128]{2,1,0:T(8,128)(2,1)S(1)}, u32[]{:S(2)}, u32[]{:S(2)}) collective-permute-start(bf16[14,64,128]{2,1,0:T(8,128)(2,1)S(1)} %get-tuple-element.28), channel_id=1, source_target_pairs={{0,2},{2,4},{4,6},{6,8},{8,10},{10,12},{12,14},{14,0},{1,3},{3,5},... | collective-permute-start | bytes 688136 | tf_op jit(solution)/shard_map/ppermute | solution.py:329
  11.0 7.3 %collective-permute-start.4 = (bf16[14,64,128]{2,1,0:T(8,128)(2,1)S(1)}, bf16[14,64,128]{2,1,0:T(8,128)(2,1)S(1)}, u32[]{:S(2)}, u32[]{:S(2)}) collective-permute-start(bf16[14,64,128]{2,1,0:T(8,128)(2,1)S(1)} %get-tuple-element.29), channel_id=1, source_target_pairs={{0,2},{2,4},{4,6},{6,8},{8,10},{10,12},{12,14},{14,0},{1,3},{3,5},... | collective-permute-start | bytes 688136 | tf_op jit(solution)/shard_map/ppermute | solution.py:340

commit v7 on v6

--- a/solution.py
+++ b/solution.py
@@ -15,7 +15,7 @@
 GROUP = 16
 REST = 16
 FIRST = 32
-EARLY = 2
+EARLY = 1
 COLUMN_BIT = 10
 SEG_BIT = 16
 UNUSED = NC_DEV * CSLOT
@@ -42,11 +42,11 @@
     return [(i, (i + by) % n) for i in range(n)]
 
 
-def prepare_kernel(n_dom, q, flat, columns, slots, counts, aggregate, requests, stiffness, picked, copied, words,
-                   last_row, columns_v, slots_v, counts_v, aggregate_v, requests_v, sems):
+def prepare_kernel(n_dom, q, flat, columns, slots, counts, aggregate, requests, picked, copied, words, columns_v,
+                    slots_v, counts_v, aggregate_v, requests_v, sems):
     rows, slot_count = columns.shape
     pairs = ((flat, copied), (requests, requests_v), (columns, columns_v), (slots, slots_v), (counts, counts_v),
-             (aggregate, aggregate_v), (stiffness.at[rows - 1], last_row))
+             (aggregate, aggregate_v))
     copies = [pltpu.make_async_copy(source, target, sems.at[i]) for i, (source, target) in enumerate(pairs)]
     for copy in copies:
         copy.start()
@@ -70,7 +70,6 @@
     words[rows : rows + 1, 0:rows] = counts_v[...]
     words[rows + 1 : rows + 2, 0:rows] = aggregate_v[...]
     words[rows + 2 : rows + 2 + n_dom, 0:q] = requests_v[0]
-    copies[6].wait()
 
 
 def block_of(word):
@@ -81,23 +80,24 @@
     return (word >> COLUMN_BIT) & (2 ** (SEG_BIT - COLUMN_BIT) - 1)
 
 
-def early_kernel(words_v, last_row, own, stiffness, words, restricted, restricted_early, row_buf, sem, sems):
-    slot_count = last_row.shape[0]
-    copy = pltpu.make_async_copy(words_v, words, sem)
-    copy.start()
-    rows = [pltpu.make_async_copy(stiffness.at[i], row_buf.at[i], sems.at[i]) for i in range(EARLY)]
-    for row in rows:
-        row.start()
-    restrict = own[own.shape[0] - 1].T
-    for k in range(slot_count):
-        restricted[k] = jnp.dot(restrict, last_row[k], preferred_element_type=f32).astype(bf16)
-    copy.wait()
-    for i in range(EARLY):
-        restrict = own[i].T
-        rows[i].wait()
+def early_kernel(words_v, own, stiffness, words, restricted, restricted_early, row_buf, sem, sems):
+    slot_count = stiffness.shape[1]
+    chosen = [stiffness.shape[0] - 1, *range(EARLY)]
+    copies = [pltpu.make_async_copy(stiffness.at[i], row_buf.at[p], sems.at[p]) for p, i in enumerate(chosen)]
+    for copy in copies:
+        copy.start()
+    word_copy = pltpu.make_async_copy(words_v, words, sem)
+    word_copy.start()
+    restrict = [own[i].T for i in chosen]
+    word_copy.wait()
+    for p, copy in enumerate(copies):
+        copy.wait()
         for k in range(slot_count):
-            y = jnp.dot(restrict, row_buf[i, k], preferred_element_type=f32)
-            restricted_early[i * slot_count + k] = y.astype(bf16)
+            y = jnp.dot(restrict[p], row_buf[p, k], preferred_element_type=f32).astype(bf16)
+            if p == 0:
+                restricted[k] = y
+            else:
+                restricted_early[(p - 1) * slot_count + k] = y
 
 
 def unfold(flat, tiles, lines, dofs):
@@ -279,16 +279,16 @@
     other_flat = lax.ppermute(own_flat, "field", [(0, 1), (1, 0)])
     n_words = -(-(rows + 2 + n_dom) // 8) * 8
     integers = lambda *shape: VMEM(shape, jnp.int32)
-    picked, own_copy, words, last_row = pl.pallas_call(
+    picked, own_copy, words = pl.pallas_call(
         functools.partial(prepare_kernel, n_dom, q),
         out_shape=(VMEM(((n_dom - 1) * q, own_flat.shape[1]), bf16), VMEM(own_flat.shape, bf16),
-                   integers(n_words, 128), VMEM((slot_count, dofs, width), bf16)),
-        in_specs=[spec(pl.ANY)] * 7,
-        out_specs=(spec(VMEM),) * 4,
+                   integers(n_words, 128)),
+        in_specs=[spec(pl.ANY)] * 6,
+        out_specs=(spec(VMEM),) * 3,
         scratch_shapes=[integers(rows, slot_count), integers(rows, slot_count), integers(1, rows), integers(1, rows),
-                        integers(1, n_dom, q), pltpu.SemaphoreType.DMA((7,))],
-        compiler_params=limit,
-    )(*map(in_hbm, (own_flat, columns, coarse_slots, counts, aggregate[None], requests, stiffness)))
+                        integers(1, n_dom, q), pltpu.SemaphoreType.DMA((6,))],
+        compiler_params=limit,
+    )(*map(in_hbm, (own_flat, columns, coarse_slots, counts, aggregate[None], requests)))
     g_own, g_other = [], []
     for s in range(1, n_dom):
         part = picked[(s - 1) * q : s * q]
@@ -305,13 +305,13 @@
         early_kernel,
         out_shape=(SMEM(words.shape, jnp.int32), VMEM((slot_count, coarse, width), bf16),
                    VMEM((EARLY * slot_count, coarse, width), bf16)),
-        in_specs=[spec(VMEM)] * 3 + [spec(pl.ANY)],
+        in_specs=[spec(VMEM)] * 2 + [spec(pl.ANY)],
         out_specs=(spec(SMEM), spec(VMEM), spec(VMEM)),
-        scratch_shapes=[VMEM((EARLY, slot_count, dofs, width), bf16), pltpu.SemaphoreType.DMA(()),
-                        pltpu.SemaphoreType.DMA((EARLY,))],
+        scratch_shapes=[VMEM((1 + EARLY, slot_count, dofs, width), bf16), pltpu.SemaphoreType.DMA(()),
+                        pltpu.SemaphoreType.DMA((1 + EARLY,))],
         compiler_params=limit,
         cost_estimate=pl.CostEstimate(flops=10**7, bytes_accessed=10**6, transcendentals=0),
-    )(in_vmem(words), in_vmem(last_row), own, in_hbm(stiffness))
+    )(in_vmem(words), own, in_hbm(stiffness))
     words = pltpu.with_memory_space_constraint(words, SMEM)
     restricted, restricted_early = in_vmem(restricted), in_vmem(restricted_early)
     acc = VMEM(block(2 * HALF), f32)

time: 19.9 us -> 20.1 us (1.010); the launches traced: 19.6 us -> 20 us
  Pallas kernels: 11.3 us -> 11.8 us
    pallas_call x1, Pallas kernels: 5.9 us -> 6.34 us  [shards(): pl.pallas_call(functools.partial(main_kernel, lead), out_shape=(VMEM(bloc...]
  transfers between devices with their start and end apart: 5 -> 5, of which waited for: 0 -> 0; matrix products, arithmetic and copies ran while one was open for 2% -> 2% of each run, Pallas kernels for 51% -> 53%
where the time goes in v7:
time: 20.1 us; the launch traced here: 20 us
  Pallas kernels  11.8 us (59%)
  starting transfers between devices  7.64 us (38%)
  local copies, waits for them, and re-layouts  0.48 us (2%)
    pallas_call x1, Pallas kernels, shards(): pl.pallas_call(functools.partial(main_kernel, lead), out_shape=(VMEM(bloc...  6.34 us
    ppermute x1, starting transfers between devices, shards(): own_part = lax.ppermute(own_part, 'blk', to_next)  2.89 us
    ppermute x1, starting transfers between devices, shards(): other_flat = lax.ppermute(own_flat, 'field', [(0, 1), (1, 0)])  2.04 us
    pallas_call x1, Pallas kernels, shards(): pl.pallas_call(early_kernel, out_shape=(SMEM(words.shape, jnp.int32), VME...  1.58 us
    ppermute x1, starting transfers between devices, shards(): other_part = lax.ppermute(other_part, 'blk', to_next)  1.35 us
    ppermute x1, starting transfers between devices, shards(): g_own.append(lax.ppermute(part, 'dom', shift_pairs(n_dom, s)))  1.31 us
    pallas_call x1, Pallas kernels, shards(): pl.pallas_call(final_kernel, out_shape=out_shape, in_specs=[spec(VMEM)] *...  1.25 us
    pallas_call x1, Pallas kernels, shards(): pl.pallas_call(functools.partial(prepare_kernel, n_dom, q), out_shape=(VM...  1.24 us
  transfers between devices with their start and end apart: 5, of which 0 were waited for; matrix products, arithmetic and copies ran while one was open for 2% of the time, Pallas kernels for 53%

profile of v7, /device:TPU:1, one launch (start us, length us, event | category | flops | bytes accessed | tf_op | source)
XLA Modules:
  0.0 20.0 jit_solution(646329785886052533)
XLA Ops:
  0.0 2.0 %collective-permute-start = (bf16[16,4096]{1,0:T(8,128)(2,1)}, bf16[16,4096]{1,0:T(8,128)(2,1)S(1)}, u32[]{:S(2)}, u32[]{:S(2)}) collective-permute-start(bf16[16,4096]{1,0:T(8,128)(2,1)} %bitcast.2), channel_id=1, source_target_pairs={{0,1},{1,0},{2,3},{3,2},{4,5},{5,4},{6,7},{7,6},{8,9},{9,8},{10,11... | collective-permute-start | bytes 393224 | tf_op jit(solution)/shard_map/ppermute | solution.py:279
  2.0 1.2 %shard_map.73 = (bf16[2,4096]{1,0:T(2,128)(2,1)S(1)}, bf16[16,4096]{1,0:T(8,128)(2,1)S(1)}, s32[24,128]{1,0:T(8,128)S(1)}) custom-call(bf16[16,4096]{1,0:T(8,128)(2,1)} %bitcast.3, s32[16,27]{1,0:T(8,128)} %columns.1, s32[16,27]{1,0:T(8,128)} %slots.1, s32[1,16]{1,0:T(1,128)} %counts.1, s32[1,16]{1,0:T(1,128)} %bitcast.4, s32[1,2,2]{2,1,0:T(2,128)} %requests.1), custom_call_target="tpu_custom_call" | custom-call | tf_op jit(solution)/shard_map/pallas_call | solution.py:282
  3.3 1.3 %collective-permute-start.2 = (bf16[2,4096]{1,0:T(2,128)(2,1)S(1)}, bf16[2,4096]{1,0:T(2,128)(2,1)S(1)}, u32[]{:S(2)}, u32[]{:S(2)}) collective-permute-start(bf16[2,4096]{1,0:T(2,128)(2,1)S(1)} %get-tuple-element.22), channel_id=1, source_target_pairs={{0,16},{16,0},{1,17},{17,1},{2,18},{18,2},{3,19},{19,3},{4,20},{20... | collective-permute-start | bytes 49160 | tf_op jit(solution)/shard_map/ppermute | solution.py:295
  4.6 0.0 collective-permute-start.1
  4.6 0.2 %reshape.6.own = bf16[16,64,64]{2,1,0:T(8,128)(2,1)S(1)} reshape(bf16[16,4096]{1,0:T(8,128)(2,1)S(1)} %get-tuple-element.18) | data formatting | bytes 262144 | tf_op jit(solution)/shard_map/reshape | solution.py:300
  4.9 1.6 %shard_map.74 = (s32[24,128]{1,0:T(8,128)S(4)}, bf16[27,64,128]{2,1,0:T(8,128)(2,1)S(1)}, bf16[27,64,128]{2,1,0:T(8,128)(2,1)S(1)}) custom-call(s32[24,128]{1,0:T(8,128)S(1)} %get-tuple-element.17.words_v, bf16[16,64,64]{2,1,0:T(8,128)(2,1)S(1)} %reshape.6.own, bf16[16,27,64,128]{3,2,1,0:T(8,128)(2,1)} %stiffness.3), custom_call_target="tpu_custom_call" | custom-call | flops 10000000 | bytes 1000000 | tf_op jit(solution)/shard_map/pallas_call | solution.py:304
  6.5 0.0 collective-permute-done.2.ghosts
  6.5 0.7 %shard_map.75 = (bf16[20,128,128]{2,1,0:T(8,128)(2,1)S(1)}, bf16[14,64,128]{2,1,0:T(8,128)(2,1)S(1)}) custom-call(s32[24,128]{1,0:T(8,128)S(4)} %get-tuple-element.19.words, bf16[27,64,128]{2,1,0:T(8,128)(2,1)S(1)} %get-tuple-element.21.restricted, bf16[16,64,64]{2,1,0:T(8,128)(2,1)S(1)} %reshape.6.own, bf16[2,4096]{1,0:T(2,128)(2,1)S(1)} %collective-permute-done.2.ghosts), custom_call_target="tpu_custom_call" | custom-call | flops 10000000 | bytes 1000000 | tf_op jit(solution)/shard_map/pallas_call | solution.py:319
  7.2 2.9 %collective-permute-start.3 = (bf16[14,64,128]{2,1,0:T(8,128)(2,1)S(1)}, bf16[14,64,128]{2,1,0:T(8,128)(2,1)S(1)}, u32[]{:S(2)}, u32[]{:S(2)}) collective-permute-start(bf16[14,64,128]{2,1,0:T(8,128)(2,1)S(1)} %get-tuple-element.26), channel_id=1, source_target_pairs={{0,2},{2,4},{4,6},{6,8},{8,10},{10,12},{12,14},{14,0},{1,3},{3,5},... | collective-permute-start | bytes 688136 | tf_op jit(solution)/shard_map/ppermute | solution.py:329
  10.1 0.0 collective-permute-done
  10.1 0.2 %reshape.7.other = bf16[16,64,64]{2,1,0:T(8,128)(2,1)S(1)} reshape(bf16[16,4096]{1,0:T(8,128)(2,1)S(1)} %collective-permute-done) | data formatting | bytes 262144 | tf_op jit(solution)/shard_map/reshape | solution.py:300
  10.3 0.0 collective-permute-done.1.ghosts
  10.4 0.7 %shard_map.76 = (bf16[20,128,128]{2,1,0:T(8,128)(2,1)S(1)}, bf16[14,64,128]{2,1,0:T(8,128)(2,1)S(1)}) custom-call(s32[24,128]{1,0:T(8,128)S(4)} %get-tuple-element.19.words, bf16[27,64,128]{2,1,0:T(8,128)(2,1)S(1)} %get-tuple-element.21.restricted, bf16[16,64,64]{2,1,0:T(8,128)(2,1)S(1)} %reshape.7.other, ...), custom_call_target="tpu_custom_call", output_to_operand_aliasing={{0}: (4, {})} | custom-call | flops 10000000 | bytes 1000000 | tf_op jit(solution)/shard_map/pallas_call | solution.py:330
  11.0 1.4 %collective-permute-start.4 = (bf16[14,64,128]{2,1,0:T(8,128)(2,1)S(1)}, bf16[14,64,128]{2,1,0:T(8,128)(2,1)S(1)}, u32[]{:S(2)}, u32[]{:S(2)}) collective-permute-start(bf16[14,64,128]{2,1,0:T(8,128)(2,1)S(1)} %get-tuple-element.27), channel_id=1, source_target_pairs={{0,2},{2,4},{4,6},{6,8},{8,10},{10,12},{12,14},{14,0},{1,3},{3,5},... | collective-permute-start | bytes 688136 | tf_op jit(solution)/shard_map/ppermute | solution.py:340
  12.4 6.3 %shard_map.77 = (bf16[3,27,64,128]{3,2,1,0:T(8,128)(2,1)S(1)}, f32[27,64,128]{2,1,0:T(8,128)S(1)}) custom-call(s32[24,128]{1,0:T(8,128)S(4)} %get-tuple-element.19.words, bf16[16,27,64,128]{3,2,1,0:T(8,128)(2,1)} %stiffness.3, bf16[16,64,64]{2,1,0:T(8,128)(2,1)S(1)} %reshape.6.own, bf16[27,64,128]{2,1,0:T(8,128)(2,1)S(1)} %get-tuple-element.20.restricted_early, ...), custom_call_target="tpu_custom_call" | custom-call | flops 1000000000 | bytes 10000000 | tf_op jit(solution)/shard_map/pallas_call | solution.py:343
  18.7 0.0 collective-permute-done.3.own_part
  18.7 0.0 collective-permute-done.4.other_part
  18.8 1.2 %shard_map.78 = bf16[4,27,64,128]{3,2,1,0:T(8,128)(2,1)} custom-call(f32[27,64,128]{2,1,0:T(8,128)S(1)} %get-tuple-element.25.partial, bf16[14,64,128]{2,1,0:T(8,128)(2,1)S(1)} %collective-permute-done.3.own_part, bf16[14,64,128]{2,1,0:T(8,128)(2,1)S(1)} %collective-permute-done.4.other_part, bf16[3,27,64,128]{3,2,1,0:T(8,128)(2,1)S(1)} %get-tuple-element.28.later_rows), custom_call_target="tpu_custom_call" | custom-call | tf_op jit(solution)/shard_map/pallas_call | solution.py:354
Async XLA Ops:
  0.0 10.1 %collective-permute-start = (bf16[16,4096]{1,0:T(8,128)(2,1)}, bf16[16,4096]{1,0:T(8,128)(2,1)S(1)}, u32[]{:S(2)}, u32[]{:S(2)}) collective-permute-start(bf16[16,4096]{1,0:T(8,128)(2,1)} %bitcast.2), channel_id=1, source_target_pairs={{0,1},{1,0},{2,3},{3,2},{4,5},{5,4},{6,7},{7,6},{8,9},{9,8},{10,11... | collective-permute-start | bytes 393224 | tf_op jit(solution)/shard_map/ppermute | solution.py:279
  3.3 3.2 %collective-permute-start.2 = (bf16[2,4096]{1,0:T(2,128)(2,1)S(1)}, bf16[2,4096]{1,0:T(2,128)(2,1)S(1)}, u32[]{:S(2)}, u32[]{:S(2)}) collective-permute-start(bf16[2,4096]{1,0:T(2,128)(2,1)S(1)} %get-tuple-element.22), channel_id=1, source_target_pairs={{0,16},{16,0},{1,17},{17,1},{2,18},{18,2},{3,19},{19,3},{4,20},{20... | collective-permute-start | bytes 49160 | tf_op jit(solution)/shard_map/ppermute | solution.py:295
  4.6 5.8 %collective-permute-start.1 = (bf16[2,4096]{1,0:T(2,128)(2,1)S(1)}, bf16[2,4096]{1,0:T(2,128)(2,1)S(1)}, u32[]{:S(2)}, u32[]{:S(2)}) collective-permute-start(bf16[2,4096]{1,0:T(2,128)(2,1)S(1)} %get-tuple-element.22), channel_id=1, source_target_pairs={{0,17},{1,16},{16,1},{17,0},{2,19},{3,18},{18,3},{19,2},{4,21},{5,... | collective-permute-start | bytes 49160 | tf_op jit(solution)/shard_map/ppermute | solution.py:297
  7.2 11.5 %collective-permute-start.3 = (bf16[14,64,128]{2,1,0:T(8,128)(2,1)S(1)}, bf16[14,64,128]{2,1,0:T(8,128)(2,1)S(1)}, u32[]{:S(2)}, u32[]{:S(2)}) collective-permute-start(bf16[14,64,128]{2,1,0:T(8,128)(2,1)S(1)} %get-tuple-element.26), channel_id=1, source_target_pairs={{0,2},{2,4},{4,6},{6,8},{8,10},{10,12},{12,14},{14,0},{1,3},{3,5},... | collective-permute-start | bytes 688136 | tf_op jit(solution)/shard_map/ppermute | solution.py:329
  11.0 7.7 %collective-permute-start.4 = (bf16[14,64,128]{2,1,0:T(8,128)(2,1)S(1)}, bf16[14,64,128]{2,1,0:T(8,128)(2,1)S(1)}, u32[]{:S(2)}, u32[]{:S(2)}) collective-permute-start(bf16[14,64,128]{2,1,0:T(8,128)(2,1)S(1)} %get-tuple-element.27), channel_id=1, source_target_pairs={{0,2},{2,4},{4,6},{6,8},{8,10},{10,12},{12,14},{14,0},{1,3},{3,5},... | collective-permute-start | bytes 688136 | tf_op jit(solution)/shard_map/ppermute | solution.py:340
